TPU v7x, 256 devices: a whole 4x4x8 slice. The times are simulated.
256 devices in a mesh: dp: 8 (over y, core), ctx: 32 (over x, z).
Axes of the slice: x: 4, y: 4, z: 8, core: 2. Of those that a mesh axis runs over, the one named last changes fastest.
Arguments:
- query_matrix_rows: bfloat16 [8, 4096, 8192], P('dp', 'ctx'), may hold values from -768 to 768
- key_matrix_rows: bfloat16 [8, 4096, 512], P('dp', 'ctx'), may hold values from -7 to 7
- value_matrix_rows: bfloat16 [8, 4096, 512], P('dp', 'ctx'), may hold values from -6 to 6
- adapter_output_gradient: bfloat16 [8, 4096, 16384], P('dp', 'ctx'), may hold values from -0.3984375 to 0.3984375
- head_output_gradient: bfloat16 [8, 4096, 8192], P('dp', 'ctx'), may hold values from -0.3984375 to 0.3984375
- sink_score_bias: float32 [64], P('ctx'), may hold values from 1 to 4
- windows: int32 [8], P('dp'), may hold values from 256 to 1024, as said below
- sink_token_count: int32 [8], P('dp'), may hold values from 1 to 16, as said below
- adapter_down_weight: bfloat16 [128, 8192], P(None, 'ctx'), may hold values from -0.0625 to 0.0625
- adapter_up_weight: bfloat16 [16384, 128], P('ctx'), may hold values from -0.5 to 0.5
Outputs:
- grad_down: float32 [128, 8192], P(None, 'ctx')
- grad_up: float32 [16384, 128], P('ctx')
- grad_bias: float32 [64], P('ctx')
Inputs may be any that keep to these rules, and one draw needn't show every extreme that they name: `windows`: some sequence has the window 1024. `sink_token_count`: some sequence has 16 sink tokens.
All inputs are finite; a program needn't handle non-finite values.
Results may differ from a plain program's by a relative error of at most 0.02.
Values may be sent and summed in bfloat16 or wider, within the bound.
A program may use at most 128 MiB of HBM per device.

v0:
```python
import jax
import jax.numpy as jnp
from jax import lax
from jax.sharding import PartitionSpec as P

HEAD_DIM = 128
WIN = 1024
SINK_MAX = 16


adapter_scale_factor = 2.0
masked = -1e30


def attend_heads(query_seq, key_seq, value_seq, grad_seq, head_bias, window_size, sink_count):
    seq_len = query_seq.shape[0]
    block_rows = min(512, seq_len)
    span = min(WIN + block_rows, seq_len)
    score_scale = HEAD_DIM ** (-0.5)
    sink_keys = key_seq[:SINK_MAX]
    sink_values = value_seq[:SINK_MAX]

    def one_block(block_index):
        query_start = block_index * block_rows
        key_start = jnp.clip(query_start + block_rows - span, 0, seq_len - span)
        query_block = lax.dynamic_slice_in_dim(query_seq, query_start, block_rows, 0)
        grad_block = lax.dynamic_slice_in_dim(grad_seq, query_start, block_rows, 0)
        local_keys = lax.dynamic_slice_in_dim(key_seq, key_start, span, 0)
        local_values = lax.dynamic_slice_in_dim(value_seq, key_start, span, 0)
        row_ids = query_start + jnp.arange(block_rows, dtype=jnp.int32)
        col_ids = key_start + jnp.arange(span, dtype=jnp.int32)
        sink_ids = jnp.arange(SINK_MAX, dtype=jnp.int32)
        local_ok = (
            (col_ids[None, :] <= row_ids[:, None])
            & (row_ids[:, None] - col_ids[None, :] < window_size)
            & (col_ids[None, :] >= sink_count)
        )
        sink_ok = (sink_ids[None, :] <= row_ids[:, None]) & (sink_ids[None, :] < sink_count)
        local_score = (
            jnp.einsum("qhd,kd->hqk", query_block, local_keys, preferred_element_type=jnp.float32)
            * score_scale
        )
        sink_score = (
            jnp.einsum("qhd,kd->hqk", query_block, sink_keys, preferred_element_type=jnp.float32)
            * score_scale
            + head_bias[:, None, None]
        )
        local_score = jnp.where(local_ok[None], local_score, masked)
        sink_score = jnp.where(sink_ok[None], sink_score, masked)
        row_max = jnp.maximum(local_score.max(-1), sink_score.max(-1))
        local_exp = jnp.exp(local_score - row_max[..., None])
        sink_exp = jnp.exp(sink_score - row_max[..., None])
        row_total = local_exp.sum(-1) + sink_exp.sum(-1)
        local_prob = local_exp / row_total[..., None]
        sink_prob = sink_exp / row_total[..., None]
        attention_head_output = jnp.einsum(
            "hqk,kd->qhd",
            local_prob.astype(jnp.bfloat16),
            local_values,
            preferred_element_type=jnp.float32,
        )
        attention_head_output = attention_head_output + jnp.einsum(
            "hqk,kd->qhd",
            sink_prob.astype(jnp.bfloat16),
            sink_values,
            preferred_element_type=jnp.float32,
        )
        attention_head_output = attention_head_output.astype(jnp.bfloat16)
        dot_sum = jnp.einsum(
            "qhd,qhd->hq", grad_block, attention_head_output, preferred_element_type=jnp.float32
        )
        sink_dot = jnp.einsum(
            "qhd,kd->hqk", grad_block, sink_values, preferred_element_type=jnp.float32
        )
        bias_part = jnp.sum(sink_prob * (sink_dot - dot_sum[:, :, None]), axis=(1, 2))
        return (attention_head_output.reshape(block_rows, -1), bias_part)

    head_outs, bias_parts = lax.map(one_block, jnp.arange(seq_len // block_rows, dtype=jnp.int32))
    return (head_outs.reshape(seq_len, -1), bias_parts.sum(0))


def on_device(
    query_matrix_rows,
    key_matrix_rows,
    value_matrix_rows,
    adapter_output_gradient,
    head_output_gradient,
    sink_score_bias,
    windows,
    sink_token_count,
    adapter_down_weight,
    adapter_up_weight,
):
    ctx_size = lax.axis_size("ctx")
    tok_rows = query_matrix_rows.shape[1]
    head_columns = adapter_down_weight.shape[1]
    per_device = head_columns // HEAD_DIM
    kv_heads = key_matrix_rows.shape[2] // HEAD_DIM
    seq_len = tok_rows * ctx_size
    grad_rows = adapter_output_gradient[0]
    columns = grad_rows
    rank_space_gradient = jnp.dot(
        columns,
        lax.all_gather(adapter_up_weight, "ctx", axis=0, tiled=True),
        preferred_element_type=jnp.float32,
    ).astype(jnp.bfloat16)
    down_weight_complete = lax.all_gather(adapter_down_weight, "ctx", axis=1, tiled=True)
    head_output_total = (
        head_output_gradient[0].astype(jnp.float32)
        + adapter_scale_factor
        * jnp.dot(rank_space_gradient, down_weight_complete, preferred_element_type=jnp.float32)
    ).astype(jnp.bfloat16)
    query_split = query_matrix_rows[0].reshape(tok_rows, ctx_size, head_columns)
    total_split = head_output_total.reshape(tok_rows, ctx_size, head_columns)
    query_heads, total_heads = (
        lax.all_to_all(query_split, "ctx", split_axis=1, concat_axis=0, tiled=True),
        lax.all_to_all(total_split, "ctx", split_axis=1, concat_axis=0, tiled=True),
    )
    key_all, value_all = (
        lax.all_gather(key_matrix_rows[0], "ctx", axis=0, tiled=True),
        lax.all_gather(value_matrix_rows[0], "ctx", axis=0, tiled=True),
    )
    kv_index = lax.axis_index("ctx") // (ctx_size // kv_heads)
    key_seq = lax.dynamic_slice_in_dim(key_all, kv_index * HEAD_DIM, HEAD_DIM, 1)
    value_seq = lax.dynamic_slice_in_dim(value_all, kv_index * HEAD_DIM, HEAD_DIM, 1)
    query_seq = query_heads.reshape(seq_len, per_device, HEAD_DIM)
    total_seq = total_heads.reshape(seq_len, per_device, HEAD_DIM)
    attention_head_output, sink_bias_gradient = attend_heads(
        query_seq, key_seq, value_seq, total_seq, sink_score_bias, windows[0], sink_token_count[0]
    )
    token_out = lax.all_to_all(
        attention_head_output.reshape(seq_len, 1, head_columns),
        "ctx",
        split_axis=0,
        concat_axis=1,
        tiled=True,
    ).reshape(tok_rows, ctx_size * head_columns)
    rank_space_output = lax.dot_general(
        token_out,
        down_weight_complete,
        (((1,), (1,)), ((), ())),
        preferred_element_type=jnp.float32,
    ).astype(jnp.bfloat16)
    down_gradient_piece = adapter_scale_factor * lax.dot_general(
        rank_space_gradient, token_out, (((0,), (0,)), ((), ())), preferred_element_type=jnp.float32
    )
    down_share = lax.psum_scatter(
        down_gradient_piece.astype(jnp.bfloat16), "ctx", scatter_dimension=1, tiled=True
    ).astype(jnp.float32)
    columns = grad_rows
    up_share = lax.psum_scatter(
        (
            adapter_scale_factor
            * lax.dot_general(
                columns,
                rank_space_output,
                (((0,), (0,)), ((), ())),
                preferred_element_type=jnp.float32,
            )
        ).astype(jnp.bfloat16),
        "ctx",
        scatter_dimension=0,
        tiled=True,
    ).astype(jnp.float32)
    up_gradient_total, down_gradient_total, bias_gradient_total = lax.psum(
        (up_share, down_share, sink_bias_gradient), "dp"
    )
    return (down_gradient_total, up_gradient_total, bias_gradient_total)


def solution(mesh):
    placed = (
        P("dp", "ctx", None),
        P("dp", "ctx", None),
        P("dp", "ctx", None),
        P("dp", "ctx", None),
        P("dp", "ctx", None),
        P("ctx"),
        P("dp"),
        P("dp"),
        P(None, "ctx"),
        P("ctx", None),
    )
    return jax.shard_map(
        on_device,
        mesh=mesh,
        in_specs=placed,
        out_specs=(P(None, "ctx"), P("ctx", None), P("ctx")),
        check_vma=False,
    )
```

profile of v0, /device:TPU:1, one launch (start us, length us, event | category | flops | bytes accessed | tf_op | source)
XLA Modules:
  0.0 1041.3 jit_solution(2569256338776049659)
XLA Ops:
  10.0 4.1 copy.25
  14.0 12.0 %all-to-all-start = ((bf16[128,32,256]{0,2,1:T(8,128)(2,1)}), bf16[128,32,256]{0,2,1:T(8,128)(2,1)}, u32[]{:S(2)}, u32[]{:S(2)}) async-start(bf16[128,32,256]{0,2,1:T(8,128)(2,1)} %bitcast.19), calls=%async_computation | async-start | bytes 4194304 | tf_op jit(solution)/shard_map/all_to_all | solution.py:116
  26.0 76.5 %all-gather.7.cloned.1.call-done = bf16[16384,128]{1,0:T(8,128)(2,1)} async-done(((bf16[512,128]{1,0:T(8,128)(2,1)}), bf16[16384,128]{1,0:T(8,128)(2,1)}) %all-gather.7.cloned.1.call-update) | async-done | bytes 4194320 | tf_op jit(solution)/shard_map/all_gather | solution.py:104
  102.6 4.7 fusion.42
  107.3 71.4 %all-gather.9.cloned.1.call-done = bf16[128,8192]{1,0:T(8,128)(2,1)} async-done(((bf16[128,256]{1,0:T(8,128)(2,1)}), bf16[128,8192]{1,0:T(8,128)(2,1)}) %all-gather.9.cloned.1.call-update) | async-done | bytes 2097168 | tf_op jit(solution)/shard_map/all_gather | solution.py:107
  178.7 2.9 fusion.38
  181.6 2.5 copy.43
  184.1 6.7 all-to-all-start.1
  191.1 4.2 copy.26
  195.3 4.2 reshape.172
  199.5 70.1 %all-gather.11.cloned.1.call-done = bf16[1,4096,512]{2,1,0:T(8,128)(2,1)} async-done(((bf16[1,128,512]{2,1,0:T(8,128)(2,1)}), bf16[1,4096,512]{2,1,0:T(8,128)(2,1)}) %all-gather.11.cloned.1.call-update) | async-done | bytes 4194320 | tf_op jit(solution)/shard_map/all_gather | solution.py:121
  270.3 81.6 %all-gather.13.cloned.1.call-done = bf16[1,4096,512]{2,1,0:T(8,128)(2,1)} async-done(((bf16[1,128,512]{2,1,0:T(8,128)(2,1)}), bf16[1,4096,512]{2,1,0:T(8,128)(2,1)}) %all-gather.13.cloned.1.call-update) | async-done | bytes 4194320 | tf_op jit(solution)/shard_map/all_gather | solution.py:120
  353.8 2.3 dynamic-slice_bitcast_fusion.1
  356.1 2.6 copy.28
  358.7 4.2 reshape.174
  362.9 126.4 %while.16 = (s32[]{:T(128)}, bf16[8,512,256]{2,1,0:T(8,128)(2,1)}, f32[8,2]{1,0:T(8,128)S(1)}, s32[8]{0:T(128)S(1)}, bf16[4096,128]{1,0:T(8,128)(2,1)}, /*index=...) while((s32[]{:T(128)}, bf16[8,512,256]{2,1,0:T(8,128)(2,1)}, ...), condition=%wide.region_6.7_spmd, body=%wide.region_0.6_spmd.sunk | while | flops 841730048 | bytes 29755260 | solution.py:78
  364.8 1.8 fusion.68
  366.7 2.4 fusion.69
  372.6 3.3 fusion.74
  380.7 1.8 fusion.68
  382.5 2.4 fusion.69
  388.4 3.3 fusion.74
  396.5 1.8 fusion.68
  398.3 2.4 fusion.69
  404.2 3.3 fusion.74
  412.3 1.8 fusion.68
  414.1 2.4 fusion.69
  420.0 3.3 fusion.74
  428.0 1.8 fusion.68
  429.9 2.4 fusion.69
  435.8 3.3 fusion.74
  445.7 2.4 fusion.69
  451.6 3.3 fusion.74
  461.5 2.4 fusion.69
  467.4 3.3 fusion.74
  477.3 2.4 fusion.69
  483.1 3.3 fusion.74
  489.8 3.9 reduce.2
  493.7 2.1 reshape.190
  495.8 49.6 %all_to_all.45 = bf16[32,2,16384]{2,1,0:T(2,128)(2,1)S(1)} all-to-all(bf16[32,2,16384]{2,1,0:T(2,128)(2,1)} %reshape.190), channel_id=1, replica_groups=mesh['dp'=8,'ctx'=32] {'ctx'}, dimensions={0} | all-to-all | bytes 4194304 | tf_op jit(solution)/shard_map/all_to_all | solution.py:131
  545.4 6.8 reshape.191
  552.2 3.9 copy.49
  556.0 3.2 copy.34
  559.3 2.1 fusion.37
  561.4 7.8 fusion.35
  569.3 208.3 %reduce-scatter.3.cloned.1.call-done = bf16[128,256]{1,0:T(8,128)(2,1)} async-done(((bf16[128,8192]{1,0:T(8,128)(2,1)}), bf16[128,256]{1,0:T(8,128)(2,1)}) %reduce-scatter.3.cloned.1.call-update) | async-done | bytes 65552 | tf_op jit(solution)/shard_map/reduce_scatter | solution.py:147
  777.5 224.7 %reduce-scatter.5.cloned.1.call-done = bf16[512,128]{0,1:T(8,128)(2,1)} async-done(((bf16[16384,128]{0,1:T(8,128)(2,1)}), bf16[512,128]{0,1:T(8,128)(2,1)}) %reduce-scatter.5.cloned.1.call-update) | async-done | bytes 131088 | tf_op jit(solution)/shard_map/reduce_scatter | solution.py:151
  1002.3 31.3 %all-reduce.2 = (f32[128,256]{1,0:T(8,128)}, f32[512,128]{0,1:T(8,128)S(1)}, f32[2]{0:T(128)}) all-reduce(bf16[128,256]{1,0:T(8,128)(2,1)} %reduce-scatter.3.cloned.1.call-done, bf16[512,128]{0,1:T(8,128)(2,1)} %reduce-scatter.5.cloned.1.call-done, f32[2]{0:T(128)S(1)} %reduce_sum.54), channel_id=1, replica_groups=mesh['dp'=8,'ctx'=32] {'dp'}, use_global_device_ids=true, to_apply=%region_8.9 | all-reduce | flops 98306 | bytes 589840 | tf_op jit(solution)/shard_map/psum | solution.py:165
  (188 shorter events, 72.2 us)
Async XLA Ops:
  7.2 95.4 %all-gather.7.cloned.1.call-start = ((), (), s32[]{:S(2)}) async-start(), calls=%async_computation.5 | async-start | bytes 4325376 | tf_op jit(solution)/shard_map/all_gather | solution.py:104
  7.9 170.8 %all-gather.9.cloned.1.call-start = ((), (), s32[]{:S(2)}) async-start(), calls=%async_computation.6 | async-start | bytes 2162688 | tf_op jit(solution)/shard_map/all_gather | solution.py:107
  8.6 261.0 %all-gather.11.cloned.1.call-start = ((), (), s32[]{:S(2)}) async-start(), calls=%async_computation.9 | async-start | bytes 4325376 | tf_op jit(solution)/shard_map/all_gather | solution.py:121
  9.4 342.5 %all-gather.13.cloned.1.call-start = ((), (), s32[]{:S(2)}) async-start(), calls=%async_computation.10 | async-start | bytes 4325376 | tf_op jit(solution)/shard_map/all_gather | solution.py:120
  14.0 170.0 %all-to-all-start = ((bf16[128,32,256]{0,2,1:T(8,128)(2,1)}), bf16[128,32,256]{0,2,1:T(8,128)(2,1)}, u32[]{:S(2)}, u32[]{:S(2)}) async-start(bf16[128,32,256]{0,2,1:T(8,128)(2,1)} %bitcast.19), calls=%async_computation | async-start | bytes 4194304 | tf_op jit(solution)/shard_map/all_to_all | solution.py:116
  184.1 172.0 %all-to-all-start.1 = ((bf16[128,32,256]{0,2,1:T(8,128)(2,1)}), bf16[128,32,256]{0,2,1:T(8,128)(2,1)S(1)}, u32[]{:S(2)}, u32[]{:S(2)}) async-start(bf16[128,32,256]{0,2,1:T(8,128)(2,1)} %bitcast.144), calls=%async_computation.1 | async-start | bytes 4194304 | tf_op jit(solution)/shard_map/all_to_all | solution.py:117
  190.8 586.8 %reduce-scatter.3.cloned.1.call-start = ((), (), s32[]{:S(2)}) async-start(), calls=%async_computation.7 | async-start | bytes 2162688 | tf_op jit(solution)/shard_map/reduce_scatter | solution.py:147
  356.1 6.8 copy-start
  561.4 440.9 %reduce-scatter.5.cloned.1.call-start = ((), (), s32[]{:S(2)}) async-start(), calls=%async_computation.8 | async-start | bytes 4325376 | tf_op jit(solution)/shard_map/reduce_scatter | solution.py:151
Sparse Core Ops, SparseCore 0:
  10.6 91.9 all-gather.6
  105.0 73.5 all-gather.8
  181.3 88.3 all-gather.10
  272.0 79.7 all-gather.12
  561.5 216.0 reduce-scatter.2
  781.8 220.4 reduce-scatter.4
where the time goes:
time: 1040 us
  waiting for transfers between devices  735 us (71%)
  blocking collectives  81 us (8%)
  matrix products  76.6 us (7%)
  local copies, waits for them, and re-layouts  66.5 us (6%)
  other arithmetic  42.5 us (4%)
  starting transfers between devices  19.1 us (2%)
  between operations  14.2 us (1%)
    reduce_scatter x1, waiting for transfers between devices, on_device(): lax.psum_scatter((adapter_scale_factor * lax.dot_general(columns, rank_sp...  225 us
    reduce_scatter x1, waiting for transfers between devices, on_device(): lax.psum_scatter(down_gradient_piece.astype(jnp.bfloat16), 'ctx', scatter...  208 us
    all_gather x1, waiting for transfers between devices, on_device(): lax.all_gather(key_matrix_rows[0], 'ctx', axis=0, tiled=True)  81.6 us
    all_gather x1, waiting for transfers between devices, on_device(): lax.all_gather(adapter_up_weight, 'ctx', axis=0, tiled=True)  76.5 us
    all_gather x1, waiting for transfers between devices, on_device(): lax.all_gather(adapter_down_weight, 'ctx', axis=1, tiled=True)  71.4 us
    all_gather x1, waiting for transfers between devices, on_device(): lax.all_gather(value_matrix_rows[0], 'ctx', axis=0, tiled=True)  70.1 us
    all_to_all x1, blocking collectives, on_device(): lax.all_to_all(attention_head_output.reshape(seq_len, 1, head_columns), '...  49.6 us
    psum x1, blocking collectives, on_device(): lax.psum((up_share, down_share, sink_bias_gradient), 'dp')  31.3 us
  transfers between devices with their start and end apart: 8, of which 6 were waited for; matrix products, arithmetic and copies ran while one was open for 3% of the time, Pallas kernels for 0%

commit v1 on v0

v1 whole, which is shorter than its diff:
```python
import jax
import jax.numpy as jnp
from jax import lax
from jax.experimental import pallas as pl
from jax.experimental.pallas import tpu as pltpu
from jax.sharding import PartitionSpec as P

NX, NY, NZ = 4, 4, 8
N_CTX, N_DP = NX * NZ, NY * 2
TOK = 128
HEAD_DIM = 128
KV_HEADS = 4
GROUP = 16
HEADS = KV_HEADS * GROUP
RANK = 128
SINKS = 16
BLOCKS = 9
UP_ROWS, DOWN_ROWS = 32, 16
CHUNK = UP_ROWS + DOWN_ROWS
HEAD_STEP = 4
MASKED = -1e30
LOG2E = 1.4426950408889634
SCORE_SCALE = LOG2E * HEAD_DIM**-0.5
BF16, F32 = jnp.bfloat16, jnp.float32
MESH = pl.DeviceIdType.MESH

ORDER = (1, 2, 3, 4, 5, 6, 7, 0, 8)
MAIN = 7 * TOK
COLS = 10 * TOK


def dot(a, b):
    return lax.dot_general(a, b, (((1,), (0,)), ((), ())), preferred_element_type=F32)


def dot_nt(a, b):
    return lax.dot_general(a, b, (((1,), (1,)), ((), ())), preferred_element_type=F32)


def kernel(
    bias_ref, win_ref, cnt_ref, q_hbm, k_hbm, v_hbm, a_hbm, h_hbm, dw_hbm, uw_hbm,
    down_out, up_out, bias_out,
    kv, sink, bb, w0, w1, q_s, a_s, h_s, o_s, t_s, kt, ve, mask,
    g0, g1, rc0, rc1, ra0, ra1, s20, s21, rb0, rb1, s3, r3, fin,
    bg, bgz, bgs, bgx, bgf,
    ld, kv_s, kv_r, sk_s, sk_r, bb_sr, w_sr, rs_sr, bg_sr,
):
    dp, ctx = lax.axis_index("dp"), lax.axis_index("ctx")
    y, c, x, z = dp // 2, dp % 2, ctx // NZ, ctx % NZ

    def dev(x_=x, y_=y, z_=z, c_=c):
        return (y_ * 2 + c_, x_ * NZ + z_)

    def off(v, i, n):
        return lax.rem(v + i + n, n)

    right, left = (dp, off(ctx, 1, N_CTX)), (dp, off(ctx, -1, N_CTX))
    jump = (dp, off(ctx, NZ, N_CTX))
    sent = []

    def rcopy(src, dst, send, recv, device):
        return pltpu.make_async_remote_copy(
            src_ref=src, dst_ref=dst, send_sem=send, recv_sem=recv, device_id=device, device_id_type=MESH
        )

    def push(src, dst, send, recv, device):
        copy = rcopy(src, dst, send, recv, device)
        copy.start()
        sent.append(copy)

    def arrived(dst, send, recv):
        rcopy(dst, dst, send, recv, right).wait_recv()

    loads = []
    for g in range(KV_HEADS):
        cols = pl.ds(g * HEAD_DIM, HEAD_DIM)
        loads.append(pltpu.make_async_copy(k_hbm.at[0, :, cols], kv.at[0, g, :, pl.ds(0, HEAD_DIM)], ld.at[2 * g]))
        loads.append(
            pltpu.make_async_copy(v_hbm.at[0, :, cols], kv.at[0, g, :, pl.ds(HEAD_DIM, HEAD_DIM)], ld.at[2 * g + 1])
        )
    own = (w0.at[c, y, x, z], w1.at[c, x, y, z])
    for half in range(2):
        rows = pl.multiple_of(dp * 2 * UP_ROWS + half * UP_ROWS, UP_ROWS)
        loads.append(
            pltpu.make_async_copy(uw_hbm.at[pl.ds(rows, UP_ROWS), :], own[half].at[pl.ds(0, UP_ROWS), :], ld.at[8 + half])
        )
        rows = pl.multiple_of(dp % 4 * 2 * DOWN_ROWS + half * DOWN_ROWS, DOWN_ROWS)
        cols = pl.multiple_of(dp // 4 * HEAD_DIM, HEAD_DIM)
        loads.append(
            pltpu.make_async_copy(
                dw_hbm.at[pl.ds(rows, DOWN_ROWS), pl.ds(cols, HEAD_DIM)],
                own[half].at[pl.ds(UP_ROWS, DOWN_ROWS), :],
                ld.at[10 + half],
            )
        )
    late = [
        pltpu.make_async_copy(q_hbm.at[0], q_s, ld.at[12]),
        pltpu.make_async_copy(a_hbm.at[0], a_s, ld.at[13]),
        pltpu.make_async_copy(h_hbm.at[0], h_s, ld.at[14]),
    ]
    for copy in loads + late:
        copy.start()

    barrier = pltpu.get_barrier_semaphore()
    partners = [left, right]
    partners += [dev(x_=off(x, i, NX)) for i in range(1, NX)]
    partners += [dev(z_=off(z, i, NZ)) for i in range(1, NZ)]
    partners += [(off(dp, i, N_DP), ctx) for i in range(1, N_DP)]
    for partner in partners:
        pl.semaphore_signal(barrier, inc=1, device_id=partner, device_id_type=MESH)
    row8 = lax.broadcasted_iota(jnp.int32, (8, HEAD_DIM), 0)
    bb[x, z] = jnp.where(row8 == 1, bias_ref[1], bias_ref[0]) * LOG2E
    for copy in loads:
        copy.wait()

    @pl.when(ctx == 0)
    def _():
        for g in range(KV_HEADS):
            sink[g] = kv[0, g, 0:SINKS, :]

    pl.semaphore_wait(barrier, len(partners))

    def kv_push(g, src, dst, device):
        push(kv.at[src, g], kv.at[dst, g], kv_s.at[dst, g], kv_r.at[dst, g], device)

    def kv_arrived(g, slot):
        arrived(kv.at[slot, g], kv_s.at[slot, g], kv_r.at[slot, g])

    for g in range(KV_HEADS):
        kv_push(g, 0, 1, right)
        kv_push(g, 0, 8, jump)

    def sink_copies(axis):
        if axis == "x":
            return [rcopy(sink, sink, sk_s.at[i], sk_r.at[0], dev(x_=off(x, i, NX))) for i in range(1, NX)]
        return [rcopy(sink, sink, sk_s.at[NX + i], sk_r.at[0], dev(z_=off(z, i, NZ))) for i in range(1, NZ)]

    @pl.when(ctx == 0)
    def _():
        for copy in sink_copies("x"):
            copy.start()

    for i in range(1, NZ):
        there = dev(z_=off(z, i, NZ))
        push(bb.at[x, z], bb.at[x, z], bb_sr.at[0, i], bb_sr.at[1, i], there)
        push(own[0], own[0], w_sr.at[0, i], w_sr.at[1, i], there)
        push(own[1], own[1], w_sr.at[0, NZ + i], w_sr.at[1, NZ + i], there)

    @pl.when(ctx != 0)
    def _():
        arrived(sink, sk_s.at[0], sk_r.at[0])

    @pl.when(z == 0)
    def _():
        for copy in sink_copies("z"):
            copy.start()

    def kv_hop(step):
        for g in range(KV_HEADS):
            kv_arrived(g, step)
            kv_push(g, step, step + 1, right)
            kv_arrived(g, 9 - step)
            kv_push(g, 9 - step, 8 - step, left)

    kv_hop(1)

    for i in range(1, NZ):
        frm = off(z, -i, NZ)
        arrived(bb.at[x, frm], bb_sr.at[0, i], bb_sr.at[1, i])
        arrived(w0.at[c, y, x, frm], w_sr.at[0, i], w_sr.at[1, i])
        arrived(w1.at[c, x, y, frm], w_sr.at[0, NZ + i], w_sr.at[1, NZ + i])
    for i in range(1, NX):
        to_x, to_y = dev(x_=off(x, i, NX)), dev(y_=off(y, i, NY))
        push(bb.at[x], bb.at[x], bb_sr.at[0, NZ + i], bb_sr.at[1, NZ + i], to_x)
        push(w0.at[c, y, x], w0.at[c, y, x], w_sr.at[0, 16 + i], w_sr.at[1, 16 + i], to_x)
        push(w1.at[c, x, y], w1.at[c, x, y], w_sr.at[0, 20 + i], w_sr.at[1, 20 + i], to_y)

    kv_hop(2)

    for i in range(1, NX):
        from_x, from_y = off(x, -i, NX), off(y, -i, NY)
        arrived(bb.at[from_x], bb_sr.at[0, NZ + i], bb_sr.at[1, NZ + i])
        arrived(w0.at[c, y, from_x], w_sr.at[0, 16 + i], w_sr.at[1, 16 + i])
        arrived(w1.at[c, x, from_y], w_sr.at[0, 20 + i], w_sr.at[1, 20 + i])
    for i in range(1, NX):
        to_x, to_y = dev(x_=off(x, i, NX)), dev(y_=off(y, i, NY))
        push(w0.at[c, y], w0.at[c, y], w_sr.at[0, 24 + i], w_sr.at[1, 24 + i], to_y)
        push(w1.at[c, x], w1.at[c, x], w_sr.at[0, 28 + i], w_sr.at[1, 28 + i], to_x)

    kv_hop(3)

    window, count = win_ref[0], cnt_ref[0]
    row = lax.broadcasted_iota(jnp.int32, (TOK, TOK), 0)
    col = lax.broadcasted_iota(jnp.int32, (TOK, TOK), 1)
    causal = col <= row

    def seen(block):
        return (block * TOK + row - col < window) & ((ctx - block) * TOK + col >= count)

    for j in range(7):
        mask[:, j * TOK : (j + 1) * TOK] = jnp.where(seen(ORDER[j]), 0.0, MASKED)
    both = jnp.where(causal, jnp.where(seen(0), 1, 0), jnp.where(seen(8), 1, 0)) == 1
    mask[:, MAIN : MAIN + TOK] = jnp.where(both, 0.0, MASKED)
    sink_seen = (col <= ctx * TOK + row) & (col < count)
    mask[:, MAIN + TOK : MAIN + 2 * TOK] = jnp.where(sink_seen, 0.0, MASKED)
    ve[:, HEAD_DIM:] = jnp.ones((COLS, HEAD_DIM), BF16)
    ve[BLOCKS * TOK :, 0:HEAD_DIM] = jnp.zeros((TOK, HEAD_DIM), BF16)
    bg[...] = jnp.zeros(bg.shape, F32)

    core_w = [
        rcopy(w.at[c], w.at[c], w_sr.at[0, 32 + half], w_sr.at[1, 32 + half], dev(c_=1 - c))
        for half, w in enumerate((w0, w1))
    ]

    late[0].wait()

    def attend_group(g, carry):
        for slot in range(4, 6):
            kv_arrived(g, slot)
        for j, block in enumerate(ORDER):
            kt[:, j * TOK : (j + 1) * TOK] = kv[block, g, :, 0:HEAD_DIM].T
            ve[j * TOK : (j + 1) * TOK, 0:HEAD_DIM] = kv[block, g, :, HEAD_DIM:]
        padded = jnp.concatenate(
            [sink[g, :, 0:HEAD_DIM], jnp.zeros((TOK - SINKS, HEAD_DIM), BF16)], axis=0
        )
        kt[:, BLOCKS * TOK :] = padded.T
        ve[BLOCKS * TOK : BLOCKS * TOK + SINKS, 0:HEAD_DIM] = sink[g, :, HEAD_DIM:]

        def attend_heads(step, carry):
            first = g * GROUP + step * HEAD_STEP
            rows = HEAD_STEP * TOK

            def columns(e):
                return pl.ds(pl.multiple_of((first + e) * HEAD_DIM, HEAD_DIM), HEAD_DIM)

            queries = jnp.concatenate([q_s[:, columns(e)] for e in range(HEAD_STEP)], axis=0)
            score = dot(queries, kt[...]) * SCORE_SCALE
            score = score.reshape(HEAD_STEP, TOK, COLS)
            parts = [
                score[:, :, j * TOK : (j + 1) * TOK] + mask[:, j * TOK : (j + 1) * TOK][None] for j in range(7)
            ]
            edge = jnp.where(causal[None], score[:, :, MAIN : MAIN + TOK], score[:, :, MAIN + TOK : MAIN + 2 * TOK])
            parts.append(edge + mask[:, MAIN : MAIN + TOK][None])
            biases = []
            for e in range(HEAD_STEP):
                head = first + e
                shard = head // 2
                biases.append(bb[shard // NZ, shard % NZ, e % 2 : e % 2 + 1, :])
            bias = jnp.concatenate([b[None] for b in biases], axis=0)
            parts.append(score[:, :, BLOCKS * TOK :] + (mask[:, MAIN + TOK : MAIN + 2 * TOK][None] + bias))
            top = parts[0]
            for part in parts[1:]:
                top = jnp.maximum(top, part)
            top = jnp.max(top, axis=-1, keepdims=True)
            probs = [jnp.exp2(part - top).astype(BF16) for part in parts]
            nothing = jnp.zeros((), BF16)
            near = jnp.where(causal[None], probs[7], nothing)
            far = jnp.where(causal[None], nothing, probs[7])
            local = jnp.concatenate(probs[:7] + [near, far], axis=-1).reshape(rows, BLOCKS * TOK)
            from_sinks = dot(probs[8].reshape(rows, TOK), ve[BLOCKS * TOK :, :])
            total = dot(local, ve[0 : BLOCKS * TOK, :]) + from_sinks
            scale = 1.0 / total[:, HEAD_DIM:]
            out = (total[:, 0:HEAD_DIM] * scale).astype(BF16)
            term = (from_sinks[:, 0:HEAD_DIM] - from_sinks[:, HEAD_DIM:] * out.astype(F32)) * scale
            for e in range(HEAD_STEP):
                o_s[:, columns(e)] = out[e * TOK : (e + 1) * TOK]
                t_s[:, columns(e)] = term[e * TOK : (e + 1) * TOK]
            return carry

        lax.fori_loop(0, GROUP // HEAD_STEP, attend_heads, 0)

        @pl.when(g == 0)
        def _():
            for i in range(1, NX):
                from_x, from_y = off(x, -i, NX), off(y, -i, NY)
                arrived(w0.at[c, from_y], w_sr.at[0, 24 + i], w_sr.at[1, 24 + i])
                arrived(w1.at[c, from_x], w_sr.at[0, 28 + i], w_sr.at[1, 28 + i])
            for copy in core_w:
                copy.start()

        return carry

    lax.fori_loop(0, KV_HEADS, attend_group, 0)

    arrived(w0.at[1 - c], w_sr.at[0, 32], w_sr.at[1, 32])
    arrived(w1.at[1 - c], w_sr.at[0, 33], w_sr.at[1, 33])
    late[1].wait()
    late[2].wait()

    pieces = [(p // 2, p % 2, half) for p in range(N_DP) for half in range(2)]

    def weight(xs, zs, piece, lo, hi):
        ys, cs, half = piece
        return w1[cs, xs, ys, zs, lo:hi, :] if half else w0[cs, ys, xs, zs, lo:hi, :]

    def low_grad_step(s, total):
        xs, zs = s // NZ, s % NZ
        up = jnp.concatenate([weight(xs, zs, piece, 0, UP_ROWS) for piece in pieces], axis=0)
        return total + dot(a_s[:, pl.ds(pl.multiple_of(s * 512, 512), 512)], up)

    low_grad = lax.fori_loop(0, N_CTX, low_grad_step, jnp.zeros((TOK, RANK), F32))
    low_grad_t = low_grad.T.astype(BF16)
    low_grad = low_grad.astype(BF16)

    def put(xs, zs, piece, lo, hi, value):
        ys, cs, half = piece
        if half:
            g1[cs, xs, ys, zs, lo:hi, :] = value
        else:
            g0[cs, ys, xs, zs, lo:hi, :] = value

    def down_step(s, total):
        xs, zs = s // NZ, s % NZ
        cols = pl.ds(pl.multiple_of(s * 256, 256), 256)
        down = jnp.concatenate(
            [
                jnp.concatenate([weight(xs, zs, piece, UP_ROWS, CHUNK) for piece in pieces[8 * e : 8 * e + 8]], axis=0)
                for e in range(2)
            ],
            axis=1,
        )
        out = o_s[:, cols]
        head_total = (h_s[:, cols].astype(F32) + 2.0 * dot(low_grad, down)).astype(BF16)
        bias_terms = jnp.sum(head_total.astype(F32) * t_s[:, cols], axis=0, keepdims=True)
        for e in range(2):
            bg[zs, xs, e : e + 1, :] = bias_terms[:, e * HEAD_DIM : (e + 1) * HEAD_DIM]
        grad = (2.0 * dot(low_grad_t, out)).astype(BF16)
        for e in range(2):
            for n, piece in enumerate(pieces[8 * e : 8 * e + 8]):
                put(
                    xs, zs, piece, UP_ROWS, CHUNK,
                    grad[n * DOWN_ROWS : (n + 1) * DOWN_ROWS, e * HEAD_DIM : (e + 1) * HEAD_DIM],
                )
        return total + dot_nt(out, down)

    low_out = lax.fori_loop(0, N_CTX, down_step, jnp.zeros((TOK, RANK), F32))
    low_out_t = low_out.T.astype(BF16)

    for i in range(1, NZ):
        push(bg.at[off(z, i, NZ)], bgz.at[i - 1], bg_sr.at[0, i], bg_sr.at[1, i], dev(z_=off(z, i, NZ)))

    def up_step(s, carry):
        xs, zs = s // NZ, s % NZ
        grad = (2.0 * dot(low_out_t, a_s[:, pl.ds(pl.multiple_of(s * 512, 512), 512)])).astype(BF16)
        for p in range(N_DP):
            for half in range(2):
                for j in range(2):
                    cols = 256 * half + 128 * j
                    put(
                        xs, zs, (p // 2, p % 2, half), 16 * j, 16 * j + 16,
                        grad[16 * p : 16 * p + 16, cols : cols + 128],
                    )
        return carry

    lax.fori_loop(0, N_CTX, up_step, 0)

    sibling = dev(c_=1 - c)
    push(g0.at[1 - c], rc0, rs_sr.at[0, 0], rs_sr.at[1, 0], sibling)
    push(g1.at[1 - c], rc1, rs_sr.at[0, 1], rs_sr.at[1, 1], sibling)

    for i in range(1, NZ):
        arrived(bgz.at[i - 1], bg_sr.at[0, i], bg_sr.at[1, i])
    terms = bg[z]
    for i in range(1, NZ):
        terms = terms + bgz[i - 1]
    bgs[...] = terms
    for i in range(1, NX):
        push(bgs.at[off(x, i, NX)], bgx.at[i - 1], bg_sr.at[0, NZ + i], bg_sr.at[1, NZ + i], dev(x_=off(x, i, NX)))

    def add_core(part, grads, received, first, second):
        arrived(received, rs_sr.at[0, part], rs_sr.at[1, part])

        def one(n, carry):
            a, b = n // second, n % second
            grads[c, a, b] = (grads[c, a, b].astype(F32) + received[a, b].astype(F32)).astype(BF16)
            return carry

        lax.fori_loop(0, first * second, one, 0)

    add_core(0, g0, rc0, NY, NX)
    for i in range(1, NY):
        push(g0.at[c, off(y, i, NY)], ra0.at[i - 1], rs_sr.at[0, 4 + i], rs_sr.at[1, 4 + i], dev(y_=off(y, i, NY)))
    add_core(1, g1, rc1, NX, NY)
    for i in range(1, NX):
        push(g1.at[c, off(x, i, NX)], ra1.at[i - 1], rs_sr.at[0, 8 + i], rs_sr.at[1, 8 + i], dev(x_=off(x, i, NX)))

    for i in range(1, NX):
        arrived(bgx.at[i - 1], bg_sr.at[0, NZ + i], bg_sr.at[1, NZ + i])
    terms = bgs[x]
    for i in range(1, NX):
        terms = terms + bgx[i - 1]
    bgf[dp] = terms
    for i in range(1, N_DP):
        push(bgf.at[dp], bgf.at[dp], bg_sr.at[0, 12 + i], bg_sr.at[1, 12 + i], (off(dp, i, N_DP), ctx))

    def add_three(grads, mine, received, result, base):
        for i in range(1, 4):
            arrived(received.at[i - 1], rs_sr.at[0, base + i], rs_sr.at[1, base + i])

        def one(n, carry):
            total = grads[c, mine, n].astype(F32)
            for i in range(3):
                total = total + received[i, n].astype(F32)
            result[n] = total.astype(BF16)
            return carry

        lax.fori_loop(0, 4, one, 0)

    add_three(g0, y, ra0, s20, 4)
    for i in range(1, NX):
        push(s20.at[off(x, i, NX)], rb0.at[i - 1], rs_sr.at[0, 12 + i], rs_sr.at[1, 12 + i], dev(x_=off(x, i, NX)))
    add_three(g1, x, ra1, s21, 8)
    for i in range(1, NY):
        push(s21.at[off(y, i, NY)], rb1.at[i - 1], rs_sr.at[0, 16 + i], rs_sr.at[1, 16 + i], dev(y_=off(y, i, NY)))

    for half, (mine, held, received) in enumerate(((x, s20, rb0), (y, s21, rb1))):
        for i in range(1, 4):
            arrived(received.at[i - 1], rs_sr.at[0, 12 + 4 * half + i], rs_sr.at[1, 12 + 4 * half + i])
        total = held[mine].astype(F32)
        for i in range(3):
            total = total + received[i].astype(F32)
        s3[:, half] = total.astype(BF16)
    for i in range(1, NZ):
        push(s3.at[off(z, i, NZ)], r3.at[i - 1], rs_sr.at[0, 20 + i], rs_sr.at[1, 20 + i], dev(z_=off(z, i, NZ)))
    for i in range(1, NZ):
        arrived(r3.at[i - 1], rs_sr.at[0, 20 + i], rs_sr.at[1, 20 + i])
    total = s3[z].astype(F32)
    for i in range(1, NZ):
        total = total + r3[i - 1].astype(F32)
    fin[dp] = total
    for i in range(1, N_DP):
        push(fin.at[dp], fin.at[dp], rs_sr.at[0, 28 + i], rs_sr.at[1, 28 + i], (off(dp, i, N_DP), ctx))

    for i in range(1, N_DP):
        frm = off(dp, -i, N_DP)
        arrived(bgf.at[frm], bg_sr.at[0, 12 + i], bg_sr.at[1, 12 + i])
    terms = bgf[0]
    for p in range(1, N_DP):
        terms = terms + bgf[p]
    bias_out[0] = jnp.sum(terms[0:1, :])
    bias_out[1] = jnp.sum(terms[1:2, :])

    for i in range(1, N_DP):
        frm = off(dp, -i, N_DP)
        arrived(fin.at[frm], rs_sr.at[0, 28 + i], rs_sr.at[1, 28 + i])
    for b in range(4):
        block = jnp.concatenate([fin[p, b // 2, 16 * (b % 2) : 16 * (b % 2) + 16, :] for p in range(N_DP)], axis=0)
        up_out[128 * b : 128 * b + 128, :] = block.T
    for e in range(2):
        block = jnp.concatenate(
            [fin[4 * e + n // 2, n % 2, UP_ROWS:CHUNK, :] for n in range(8)], axis=0
        )
        down_out[:, e * HEAD_DIM : (e + 1) * HEAD_DIM] = block

    for copy in sent + core_w:
        copy.wait_send()

    @pl.when(ctx == 0)
    def _():
        for copy in sink_copies("x"):
            copy.wait_send()

    @pl.when(z == 0)
    def _():
        for copy in sink_copies("z"):
            copy.wait_send()


def on_device(q, k, v, a, h, bias, windows, counts, down, up):
    hbm, smem, vmem = (pl.BlockSpec(memory_space=s) for s in (pl.ANY, pltpu.SMEM, pltpu.VMEM))
    sem = pltpu.SemaphoreType.DMA
    chunk = (CHUNK, HEAD_DIM)
    heads = HEADS * HEAD_DIM
    scratch = [
        pltpu.VMEM((BLOCKS, KV_HEADS, TOK, 2 * HEAD_DIM), BF16),
        pltpu.VMEM((KV_HEADS, SINKS, 2 * HEAD_DIM), BF16),
        pltpu.VMEM((NX, NZ, 8, HEAD_DIM), F32),
        pltpu.VMEM((2, NY, NX, NZ) + chunk, BF16),
        pltpu.VMEM((2, NX, NY, NZ) + chunk, BF16),
        pltpu.VMEM((TOK, heads), BF16),
        pltpu.VMEM((TOK, a.shape[2]), BF16),
        pltpu.VMEM((TOK, heads), BF16),
        pltpu.VMEM((TOK, heads), BF16),
        pltpu.VMEM((TOK, heads), F32),
        pltpu.VMEM((HEAD_DIM, COLS), BF16),
        pltpu.VMEM((COLS, 2 * HEAD_DIM), BF16),
        pltpu.VMEM((TOK, BLOCKS * TOK), F32),
        pltpu.VMEM((2, NY, NX, NZ) + chunk, BF16),
        pltpu.VMEM((2, NX, NY, NZ) + chunk, BF16),
        pltpu.VMEM((NY, NX, NZ) + chunk, BF16),
        pltpu.VMEM((NX, NY, NZ) + chunk, BF16),
        pltpu.VMEM((3, NX, NZ) + chunk, BF16),
        pltpu.VMEM((3, NY, NZ) + chunk, BF16),
        pltpu.VMEM((NX, NZ) + chunk, BF16),
        pltpu.VMEM((NY, NZ) + chunk, BF16),
        pltpu.VMEM((3, NZ) + chunk, BF16),
        pltpu.VMEM((3, NZ) + chunk, BF16),
        pltpu.VMEM((NZ, 2) + chunk, BF16),
        pltpu.VMEM((NZ - 1, 2) + chunk, BF16),
        pltpu.VMEM((N_DP, 2) + chunk, F32),
        pltpu.VMEM((NZ, NX, 8, HEAD_DIM), F32),
        pltpu.VMEM((NZ - 1, NX, 8, HEAD_DIM), F32),
        pltpu.VMEM((NX, 8, HEAD_DIM), F32),
        pltpu.VMEM((NX - 1, 8, HEAD_DIM), F32),
        pltpu.VMEM((N_DP, 8, HEAD_DIM), F32),
        sem((15,)),
        sem((BLOCKS, KV_HEADS)),
        sem((BLOCKS, KV_HEADS)),
        sem((NX + NZ,)),
        sem((1,)),
        sem((2, NZ + NX)),
        sem((2, 34)),
        sem((2, 36)),
        sem((2, 20)),
    ]
    return pl.pallas_call(
        kernel,
        out_shape=(
            jax.ShapeDtypeStruct(down.shape, F32),
            jax.ShapeDtypeStruct(up.shape, F32),
            jax.ShapeDtypeStruct(bias.shape, F32),
        ),
        in_specs=[smem] * 3 + [hbm] * 7,
        out_specs=(vmem, vmem, smem),
        scratch_shapes=scratch,
        compiler_params=pltpu.CompilerParams(
            collective_id=0, has_side_effects=True, vmem_limit_bytes=60 * 1024 * 1024
        ),
        name="token_parallel",
    )(bias, windows, counts, q, k, v, a, h, down, up)


def solution(mesh):
    rows = P("dp", "ctx", None)
    placed = (rows,) * 5 + (P("ctx"), P("dp"), P("dp"), P(None, "ctx"), P("ctx", None))
    return jax.shard_map(
        on_device,
        mesh=mesh,
        in_specs=placed,
        out_specs=(P(None, "ctx"), P("ctx", None), P("ctx")),
        check_vma=False,
    )
```

time: 1040 us -> 172 us (0.17)
  waiting for transfers between devices: 735 us -> 0 us
  Pallas kernels: 0 us -> 165 us
  blocking collectives: 81 us -> 0 us
  matrix products: 76.6 us -> 0 us
  local copies, waits for them, and re-layouts: 66.5 us -> 4.35 us
  other arithmetic: 42.5 us -> 0 us
  starting transfers between devices: 19.1 us -> 0 us
  between operations: 14.2 us -> 1.93 us
    reduce_scatter x2 -> x0, waiting for transfers between devices: 433 us -> none  [the longest x1 225 us: on_device(): lax.psum_scatter((adapter_scale_factor * lax.dot_general(columns, rank_sp...]
    all_gather x4 -> x0, waiting for transfers between devices: 300 us -> none  [the longest x1 81.6 us: on_device(): lax.all_gather(key_matrix_rows[0], 'ctx', axis=0, tiled=True)]
    pallas_call x0 -> x1, Pallas kernels: none -> 165 us  [on_device(): pl.pallas_call(kernel, out_shape=(jax.ShapeDtypeStruct(down.shape, F32),...]
    dot_general x44 -> x0, matrix products: 76.6 us -> none  [the longest x8 26.4 us: one_block(): jnp.einsum('hqk,kd->qhd', local_prob.astype(jnp.bfloat16), local_values,...]
    all_to_all x1 -> x0, blocking collectives: 49.6 us -> none  [on_device(): lax.all_to_all(attention_head_output.reshape(seq_len, 1, head_columns), '...]
    psum x1 -> x0, blocking collectives: 31.3 us -> none  [on_device(): lax.psum((up_share, down_share, sink_bias_gradient), 'dp')]
    all_to_all x2 -> x0, starting transfers between devices: 18.7 us -> none  [the longest x1 12 us: on_device(): lax.all_to_all(query_split, 'ctx', split_axis=1, concat_axis=0, tiled=True)]
    dynamic_slice x26 -> x0, local copies, waits for them, and re-layouts: 17.4 us -> none  [the longest x16 9.15 us: one_block(): grad_block = lax.dynamic_slice_in_dim(grad_seq, query_start, block_rows, 0)]
  transfers between devices with their start and end apart: 8 -> 0, of which waited for: 6 -> 0; matrix products, arithmetic and copies ran while one was open for 3% -> 0% of each run, Pallas kernels for 0% -> 0%
where the time goes in v1:
time: 172 us; the launch traced here: 171 us
  Pallas kernels  165 us (96%)
  local copies, waits for them, and re-layouts  4.35 us (3%)
  between operations  1.93 us (1%)
    pallas_call x1, Pallas kernels, on_device(): pl.pallas_call(kernel, out_shape=(jax.ShapeDtypeStruct(down.shape, F32),...  165 us
    unnamed x3, local copies, waits for them, and re-layouts  4.35 us

profile of v1, /device:TPU:1, one launch (start us, length us, event | category | flops | bytes accessed | tf_op | source)
XLA Modules:
  0.0 171.4 jit_solution(7217723251610049917)
XLA Ops:
  1.9 165.1 %token_parallel.1 = (f32[128,256]{1,0:T(8,128)}, f32[512,128]{1,0:T(8,128)}, f32[2]{0:T(128)}) custom-call(f32[2]{0:T(128)} %bias_ref.1, s32[1]{0:T(128)S(6)} %copy.16.win_ref, s32[1]{0:T(128)S(6)} %copy.17.cnt_ref, bf16[1,128,8192]{2,1,0:T(8,128)(2,1)} %q_hbm.1, bf16[1,128,512]{2,1,0:T(8,128)(2,1)} %k_hbm.1, bf16[1,128,512]{2,1,0:T(8,128)(2,1)} %v_hbm.1, ...), custom_call_target="tpu_custom_call" | custom-call | tf_op jit(solution)/shard_map/token_parallel/pallas_call | solution.py:516
  167.0 1.6 copy.18
  168.6 1.7 copy.19
  170.3 1.1 copy.20

commit v2 on v1

v2 whole, which is shorter than its diff:
```python
import jax
import jax.numpy as jnp
from jax import lax
from jax.experimental import pallas as pl
from jax.experimental.pallas import tpu as pltpu
from jax.sharding import PartitionSpec as P

NX, NY, NZ = 4, 4, 8
N_CTX, N_DP = NX * NZ, NY * 2
TOK = 128
HEAD_DIM = 128
KV_HEADS = 4
GROUP = 16
HEADS = KV_HEADS * GROUP
RANK = 128
SINKS = 16
BLOCKS = 9
UP_ROWS, DOWN_ROWS = 32, 16
HEAD_STEP = 4
MASKED = -1e30
LOG2E = 1.4426950408889634
SCORE_SCALE = LOG2E * HEAD_DIM**-0.5
BF16, F32 = jnp.bfloat16, jnp.float32
MESH = pl.DeviceIdType.MESH

ORDER = (1, 2, 3, 4, 5, 6, 7, 0, 8)
MAIN = 7 * TOK
COLS = 10 * TOK


def dot(a, b):
    return lax.dot_general(a, b, (((1,), (0,)), ((), ())), preferred_element_type=F32)


def dot_nt(a, b):
    return lax.dot_general(a, b, (((1,), (1,)), ((), ())), preferred_element_type=F32)


def kernel(
    bias_ref, win_ref, cnt_ref, q_hbm, k_hbm, v_hbm, a_hbm, h_hbm, dw_hbm, uw_hbm,
    fin_u_out, fin_d_out, bias_out,
    kv, sink, bb, wu, wd, q_s, a_s, h_s, o_s, t_s, kt, ve, mask,
    gu, gd, rcu, rcd, rau, rad, s2u, s2d, rbu, rbd, s3u, s3d, r3u, r3d, finu, find,
    bg, bgz, bgs, bgx, bgf,
    ld, kv_s, kv_r, sk, bb_s, bb_r, w_s, w_r, rs_s, rs_r, bg_s, bg_r,
):
    dp, ctx = lax.axis_index("dp"), lax.axis_index("ctx")
    y, c, x, z = dp // 2, dp % 2, ctx // NZ, ctx % NZ

    def dev(x_=x, y_=y, z_=z, c_=c):
        return (y_ * 2 + c_, x_ * NZ + z_)

    def off(v, i, n):
        return lax.rem(v + i + n, n)

    right, left = (dp, off(ctx, 1, N_CTX)), (dp, off(ctx, -1, N_CTX))
    jump = (dp, off(ctx, NZ, N_CTX))
    sibling = dev(c_=1 - c)

    def rcopy(src, dst, send, recv, device):
        return pltpu.make_async_remote_copy(
            src_ref=src, dst_ref=dst, send_sem=send, recv_sem=recv, device_id=device, device_id_type=MESH
        )

    def push(src, dst, send, recv, device):
        rcopy(src, dst, send, recv, device).start()

    def arrived(ref, recv):
        rcopy(ref, ref, recv, recv, right).wait_recv()

    def left_here(ref, send):
        rcopy(ref, ref, send, send, right).wait_send()

    for g in range(KV_HEADS):
        cols = pl.ds(g * HEAD_DIM, HEAD_DIM)
        pltpu.make_async_copy(k_hbm.at[0, :, cols], kv.at[0, g, :, pl.ds(0, HEAD_DIM)], ld.at[0]).start()
        pltpu.make_async_copy(v_hbm.at[0, :, cols], kv.at[0, g, :, pl.ds(HEAD_DIM, HEAD_DIM)], ld.at[0]).start()
    for half in range(2):
        rows = pl.multiple_of(dp % 4 * 2 * DOWN_ROWS + half * DOWN_ROWS, DOWN_ROWS)
        cols = pl.multiple_of(dp // 4 * HEAD_DIM, HEAD_DIM)
        pltpu.make_async_copy(
            dw_hbm.at[pl.ds(rows, DOWN_ROWS), pl.ds(cols, HEAD_DIM)], wd.at[half, c, x, y, z], ld.at[1]
        ).start()
        rows = pl.multiple_of(dp * 2 * UP_ROWS + half * UP_ROWS, UP_ROWS)
        pltpu.make_async_copy(uw_hbm.at[pl.ds(rows, UP_ROWS), :], wu.at[half, c, x, y, z], ld.at[2]).start()
    late = [
        pltpu.make_async_copy(q_hbm.at[0], q_s, ld.at[3]),
        pltpu.make_async_copy(a_hbm.at[0], a_s, ld.at[4]),
        pltpu.make_async_copy(h_hbm.at[0], h_s, ld.at[5]),
    ]
    for copy in late:
        copy.start()

    barrier = pltpu.get_barrier_semaphore()
    partners = [left, right]
    partners += [dev(x_=off(x, i, NX)) for i in range(1, NX)]
    partners += [dev(z_=off(z, i, NZ)) for i in range(1, NZ)]
    partners += [(off(dp, i, N_DP), ctx) for i in range(1, N_DP)]
    for partner in partners:
        pl.semaphore_signal(barrier, inc=1, device_id=partner, device_id_type=MESH)
    row8 = lax.broadcasted_iota(jnp.int32, (8, HEAD_DIM), 0)
    bb[x, z] = jnp.where(row8 == 1, bias_ref[1], bias_ref[0]) * LOG2E
    for n, ref in enumerate((kv.at[0], wd.at[:, c, x, y, z], wu.at[:, c, x, y, z])):
        pltpu.make_async_copy(ref, ref, ld.at[n]).wait()

    @pl.when(ctx == 0)
    def _():
        for g in range(KV_HEADS):
            sink[g] = kv[0, g, 0:SINKS, :]

    pl.semaphore_wait(barrier, len(partners))

    first_z = z == 0
    far_slot = jnp.where(first_z, 7, 8)
    far_device = (dp, jnp.where(first_z, x * NZ + NZ - 1, off(ctx, NZ, N_CTX)))

    def kv_push(g, src, dst, device):
        push(kv.at[src, g], kv.at[dst, g], kv_s.at[0], kv_r.at[dst, g], device)

    def kv_arrived(g, slot):
        arrived(kv.at[slot, g], kv_r.at[slot, g])

    def kv_hop(step):
        for g in range(KV_HEADS):
            kv_arrived(g, step)
            kv_push(g, step, step + 1, right)
            if step == 1:

                @pl.when(z != 0)
                def _():
                    kv_arrived(g, 8)
                    kv_push(g, 8, 7, left)

            else:
                kv_arrived(g, 9 - step)
                kv_push(g, 9 - step, 8 - step, left)

    for g in range(KV_HEADS):
        kv_push(g, 0, 1, right)
        kv_push(g, 0, far_slot, far_device)

    def sink_copies(axis):
        if axis == "x":
            return [rcopy(sink, sink, sk.at[0], sk.at[2], dev(x_=off(x, i, NX))) for i in range(1, NX)]
        return [rcopy(sink, sink, sk.at[1], sk.at[2], dev(z_=off(z, i, NZ))) for i in range(1, NZ)]

    @pl.when(ctx == 0)
    def _():
        for copy in sink_copies("x"):
            copy.start()

    weights = (wd, wu)

    def w_push(part, stage, src, device):
        push(src, src, w_s.at[part, stage], w_r.at[part, stage], device)

    w_sizes = [
        (w.at[0, c, 0, pl.ds(0, 2), pl.ds(0, 7)], w.at[0, c, pl.ds(0, 3), pl.ds(0, 2)], w.at[:, c, pl.ds(0, 3)], w.at[:, c])
        for w in weights
    ]

    def w_arrived(part, stage):
        arrived(w_sizes[part][stage], w_r.at[part, stage])

    def along_z(part):
        for i in range(1, NZ):
            w_push(part, 0, weights[part].at[:, c, x, y, z], dev(z_=off(z, i, NZ)))

    def second(part):
        w = weights[part]
        for i in range(1, NX):
            if part == 0:
                w_push(part, 1, w.at[:, c, x, y], dev(x_=off(x, i, NX)))
            else:
                w_push(part, 1, w.at[0, c, x, y], dev(x_=off(x, i, NX)))
                w_push(part, 1, w.at[1, c, x, y], dev(y_=off(y, i, NY)))

    def third(part, half):
        w = weights[part]
        for i in range(1, NX):
            if part == 1 and half == 1:
                w_push(part, 2, w.at[1, c, x], dev(x_=off(x, i, NX)))
            else:
                w_push(part, 2, w.at[half, c, :, y], dev(y_=off(y, i, NY)))

    def core(part):
        w_push(part, 3, weights[part].at[:, c], sibling)

    for i in range(1, NZ):
        push(bb.at[x, z], bb.at[x, z], bb_s.at[0], bb_r.at[0], dev(z_=off(z, i, NZ)))
    along_z(0)
    along_z(1)

    window, count = win_ref[0], cnt_ref[0]
    row = lax.broadcasted_iota(jnp.int32, (TOK, TOK), 0)
    col = lax.broadcasted_iota(jnp.int32, (TOK, TOK), 1)
    causal = col <= row

    def seen(block):
        return (block * TOK + row - col < window) & ((ctx - block) * TOK + col >= count)

    for j in range(7):
        mask[:, j * TOK : (j + 1) * TOK] = jnp.where(seen(ORDER[j]), 0.0, MASKED)
    both = jnp.where(causal, jnp.where(seen(0), 1, 0), jnp.where(seen(8), 1, 0)) == 1
    mask[:, MAIN : MAIN + TOK] = jnp.where(both, 0.0, MASKED)
    sink_seen = (col <= ctx * TOK + row) & (col < count)
    mask[:, MAIN + TOK : MAIN + 2 * TOK] = jnp.where(sink_seen, 0.0, MASKED)
    ve[:, HEAD_DIM:] = jnp.ones((COLS, HEAD_DIM), BF16)
    ve[BLOCKS * TOK :, 0:HEAD_DIM] = jnp.zeros((TOK, HEAD_DIM), BF16)
    bg[...] = jnp.zeros(bg.shape, F32)

    kv_hop(1)

    @pl.when((z == 0) & (x != 0))
    def _():
        arrived(sink, sk.at[2])

    @pl.when(z == 0)
    def _():
        for copy in sink_copies("z"):
            copy.start()

    arrived(bb.at[0, pl.ds(0, 7)], bb_r.at[0])
    for i in range(1, NX):
        push(bb.at[x], bb.at[x], bb_s.at[1], bb_r.at[1], dev(x_=off(x, i, NX)))
    w_arrived(0, 0)
    second(0)

    kv_hop(2)

    w_arrived(1, 0)
    second(1)
    w_arrived(0, 1)
    third(0, 0)
    third(0, 1)

    kv_hop(3)

    @pl.when(first_z)
    def _():
        for g in range(KV_HEADS):
            kv_push(g, 0, 8, jump)

    w_arrived(1, 1)
    third(1, 0)
    arrived(bb.at[pl.ds(0, 3)], bb_r.at[1])

    @pl.when(z != 0)
    def _():
        arrived(sink, sk.at[2])

    late[0].wait()

    def attend_group(g, carry):
        kv_arrived(g, 4)
        kv_arrived(g, 5)

        @pl.when(first_z)
        def _():
            kv_arrived(g, 8)

        for j, block in enumerate(ORDER):
            kt[:, j * TOK : (j + 1) * TOK] = kv[block, g, :, 0:HEAD_DIM].T
            ve[j * TOK : (j + 1) * TOK, 0:HEAD_DIM] = kv[block, g, :, HEAD_DIM:]
        padded = jnp.concatenate(
            [sink[g, :, 0:HEAD_DIM], jnp.zeros((TOK - SINKS, HEAD_DIM), BF16)], axis=0
        )
        kt[:, BLOCKS * TOK :] = padded.T
        ve[BLOCKS * TOK : BLOCKS * TOK + SINKS, 0:HEAD_DIM] = sink[g, :, HEAD_DIM:]

        def attend_heads(step, carry):
            first = g * GROUP + step * HEAD_STEP
            rows = HEAD_STEP * TOK

            def columns(e):
                return pl.ds(pl.multiple_of((first + e) * HEAD_DIM, HEAD_DIM), HEAD_DIM)

            queries = jnp.concatenate([q_s[:, columns(e)] for e in range(HEAD_STEP)], axis=0)
            score = dot(queries, kt[...]) * SCORE_SCALE
            score = score.reshape(HEAD_STEP, TOK, COLS)
            parts = [
                score[:, :, j * TOK : (j + 1) * TOK] + mask[:, j * TOK : (j + 1) * TOK][None] for j in range(7)
            ]
            edge = jnp.where(causal[None], score[:, :, MAIN : MAIN + TOK], score[:, :, MAIN + TOK : MAIN + 2 * TOK])
            parts.append(edge + mask[:, MAIN : MAIN + TOK][None])
            biases = []
            for e in range(HEAD_STEP):
                head = first + e
                shard = head // 2
                biases.append(bb[shard // NZ, shard % NZ, e % 2 : e % 2 + 1, :])
            bias = jnp.concatenate([b[None] for b in biases], axis=0)
            parts.append(score[:, :, BLOCKS * TOK :] + (mask[:, MAIN + TOK : MAIN + 2 * TOK][None] + bias))
            top = parts[0]
            for part in parts[1:]:
                top = jnp.maximum(top, part)
            top = jnp.max(top, axis=-1, keepdims=True)
            probs = [jnp.exp2(part - top).astype(BF16) for part in parts]
            nothing = jnp.zeros((), BF16)
            near = jnp.where(causal[None], probs[7], nothing)
            far = jnp.where(causal[None], nothing, probs[7])
            local = jnp.concatenate(probs[:7] + [near, far], axis=-1).reshape(rows, BLOCKS * TOK)
            from_sinks = dot(probs[8].reshape(rows, TOK), ve[BLOCKS * TOK :, :])
            total = dot(local, ve[0 : BLOCKS * TOK, :]) + from_sinks
            scale = 1.0 / total[:, HEAD_DIM:]
            out = (total[:, 0:HEAD_DIM] * scale).astype(BF16)
            term = (from_sinks[:, 0:HEAD_DIM] - from_sinks[:, HEAD_DIM:] * out.astype(F32)) * scale
            for e in range(HEAD_STEP):
                o_s[:, columns(e)] = out[e * TOK : (e + 1) * TOK]
                t_s[:, columns(e)] = term[e * TOK : (e + 1) * TOK]
            return carry

        lax.fori_loop(0, GROUP // HEAD_STEP, attend_heads, 0)

        @pl.when(g == 0)
        def _():
            third(1, 1)

        @pl.when(g == 2)
        def _():
            w_arrived(0, 2)
            core(0)

        return carry

    lax.fori_loop(0, KV_HEADS, attend_group, 0)

    pieces = [(half, p % 2, p // 2) for p in range(N_DP) for half in range(2)]

    def down_weight(xs, zs):
        return [
            jnp.concatenate([wd[half, cs, xs, ys, zs] for half, cs, ys in pieces[8 * e : 8 * e + 8]], axis=0)
            for e in range(2)
        ]

    w_arrived(0, 3)

    def low_out_step(xs, total):
        down = jnp.concatenate([w for zs in range(NZ) for w in down_weight(xs, zs)], axis=1)
        return total + dot_nt(down, o_s[:, pl.ds(pl.multiple_of(xs * 2048, 2048), 2048)])

    low_out_t = lax.fori_loop(0, NX, low_out_step, jnp.zeros((RANK, TOK), F32)).astype(BF16)
    late[1].wait()

    grads, from_core = (gd, gu), (rcd, rcu)
    first_in, first_sum = (rad, rau), (s2d, s2u)
    second_in, second_sum = (rbd, rbu), (s3d, s3u)
    third_in, final = (r3d, r3u), (find, finu)
    order = [off(x, i, NX) for i in (1, 2, 3, 0)]

    CORE, FIRST, SECOND, THIRD, LAST = 0, 4, 5, 6, 7
    rs_sizes = [
        {CORE: from_core[p], FIRST: first_in[p], SECOND: second_in[p], THIRD: third_in[p], LAST: final[p].at[pl.ds(0, 7)]}
        for p in range(2)
    ]

    def rs_push(part, stage, src, dst, device, row=0):
        push(src, dst, rs_s.at[part, stage], rs_r.at[part, stage + row], device)

    def rs_arrived(part, stage):
        arrived(rs_sizes[part][stage], rs_r.at[part, stage])

    def to_core(part, j):
        xs = order[j]
        rs_push(part, CORE, grads[part].at[:, 1 - c, xs], from_core[part].at[:, xs], sibling, j)

    def first_stage(part, j):
        xs = order[j]
        arrived(from_core[part].at[:, xs], rs_r.at[part, j])
        mine, theirs = grads[part], from_core[part]

        def one(n, carry):
            half, ys = n // NY, n % NY
            mine[half, c, xs, ys] = (mine[half, c, xs, ys].astype(F32) + theirs[half, xs, ys].astype(F32)).astype(BF16)
            return carry

        lax.fori_loop(0, 2 * NY, one, 0)
        for i in range(1, NY):
            rs_push(part, FIRST, mine.at[0, c, xs, off(y, i, NY)], first_in[part].at[0, i - 1, xs], dev(y_=off(y, i, NY)))
        if j < 3:
            rs_push(part, FIRST, mine.at[1, c, xs], first_in[part].at[1, j], dev(x_=xs))

    def second_stage(part):
        rs_arrived(part, FIRST)
        mine, theirs, total = grads[part], first_in[part], first_sum[part]

        def one(n, carry):
            for half, own in ((0, mine.at[0, c, n, y]), (1, mine.at[1, c, x, n])):
                acc = own[...].astype(F32)
                for i in range(3):
                    acc = acc + theirs[half, i, n].astype(F32)
                total[half, n] = acc.astype(BF16)
            return carry

        lax.fori_loop(0, 4, one, 0)
        for i in range(1, NX):
            to_x, to_y = off(x, i, NX), off(y, i, NY)
            rs_push(part, SECOND, total.at[0, to_x], second_in[part].at[0, i - 1], dev(x_=to_x))
            rs_push(part, SECOND, total.at[1, to_y], second_in[part].at[1, i - 1], dev(y_=to_y))

    def third_stage(part):
        rs_arrived(part, SECOND)
        mine, theirs, total = first_sum[part], second_in[part], second_sum[part]
        for half, own in ((0, x), (1, y)):
            acc = mine[half, own].astype(F32)
            for i in range(3):
                acc = acc + theirs[half, i].astype(F32)
            total[:, half] = acc.astype(BF16)
        for i in range(1, NZ):
            rs_push(part, THIRD, total.at[off(z, i, NZ)], third_in[part].at[i - 1], dev(z_=off(z, i, NZ)))

    def last_stage(part):
        rs_arrived(part, THIRD)
        acc = second_sum[part][z].astype(F32)
        for i in range(1, NZ):
            acc = acc + third_in[part][i - 1].astype(F32)
        final[part][dp] = acc.astype(BF16)
        for i in range(1, N_DP):
            rs_push(part, LAST, final[part].at[dp], final[part].at[dp], (off(dp, i, N_DP), ctx))

    def last_arrived(part):
        rs_arrived(part, LAST)

    def up_row(xs):
        def step(zs, carry):
            cols = pl.ds(pl.multiple_of((xs * NZ + zs) * 512, 512), 512)
            grad = (2.0 * dot(low_out_t, a_s[:, cols])).astype(BF16)
            for p in range(N_DP):
                for half in range(2):
                    for j in range(2):
                        lane = 256 * half + 128 * j
                        gu[half, p % 2, xs, p // 2, zs, 16 * j : 16 * j + 16, :] = grad[
                            16 * p : 16 * p + 16, lane : lane + 128
                        ]
            return carry

        lax.fori_loop(0, NZ, step, 0, unroll=2)

    for j in range(NX):
        up_row(order[j])
        to_core(1, j)
        if j > 0:
            first_stage(1, j - 1)
        if j == 2:
            w_arrived(1, 2)
            core(1)
    first_stage(1, 3)

    w_arrived(1, 3)

    def low_grad_step(xs, total):
        up = jnp.concatenate(
            [wu[half, cs, xs, ys, zs] for zs in range(NZ) for half, cs, ys in pieces], axis=0
        )
        return total + dot(a_s[:, pl.ds(pl.multiple_of(xs * 4096, 4096), 4096)], up)

    low_grad = lax.fori_loop(0, NX, low_grad_step, jnp.zeros((TOK, RANK), F32))
    low_grad_t = low_grad.T.astype(BF16)
    low_grad = low_grad.astype(BF16)
    late[2].wait()

    def down_row(xs):
        def step(zs, carry):
            cols = pl.ds(pl.multiple_of((xs * NZ + zs) * 256, 256), 256)
            down = jnp.concatenate(down_weight(xs, zs), axis=1)
            head_total = (h_s[:, cols].astype(F32) + 2.0 * dot(low_grad, down)).astype(BF16)
            bias_terms = jnp.sum(head_total.astype(F32) * t_s[:, cols], axis=0, keepdims=True)
            for e in range(2):
                bg[zs, xs, e : e + 1, :] = bias_terms[:, e * HEAD_DIM : (e + 1) * HEAD_DIM]
            grad = (2.0 * dot(low_grad_t, o_s[:, cols])).astype(BF16)
            for n, (half, cs, ys) in enumerate(pieces):
                e, r = n // 8, n % 8 * DOWN_ROWS
                gd[half, cs, xs, ys, zs] = grad[r : r + DOWN_ROWS, e * HEAD_DIM : (e + 1) * HEAD_DIM]
            return carry

        lax.fori_loop(0, NZ, step, 0, unroll=2)

    for j in range(NX):
        down_row(order[j])
        to_core(0, j)
        if j > 0:
            first_stage(0, j - 1)

    for i in range(1, NZ):
        push(bg.at[off(z, i, NZ)], bgz.at[i - 1], bg_s.at[0], bg_r.at[0], dev(z_=off(z, i, NZ)))
    first_stage(0, 3)
    second_stage(1)

    arrived(bgz, bg_r.at[0])
    terms = bg[z]
    for i in range(1, NZ):
        terms = terms + bgz[i - 1]
    bgs[...] = terms
    for i in range(1, NX):
        push(bgs.at[off(x, i, NX)], bgx.at[i - 1], bg_s.at[1], bg_r.at[1], dev(x_=off(x, i, NX)))

    second_stage(0)
    third_stage(1)

    arrived(bgx, bg_r.at[1])
    terms = bgs[x]
    for i in range(1, NX):
        terms = terms + bgx[i - 1]
    bgf[dp] = terms
    for i in range(1, N_DP):
        push(bgf.at[dp], bgf.at[dp], bg_s.at[2], bg_r.at[2], (off(dp, i, N_DP), ctx))

    third_stage(0)
    last_stage(1)
    last_stage(0)

    arrived(bgf.at[pl.ds(0, 7)], bg_r.at[2])
    terms = bgf[0]
    for p in range(1, N_DP):
        terms = terms + bgf[p]
    bias_out[...] = terms
    last_arrived(1)
    fin_u_out[...] = finu[...]
    last_arrived(0)
    fin_d_out[...] = find[...]

    left_here(kv.at[pl.ds(1, 8)], kv_s.at[0])
    left_here(bb.at[0, pl.ds(0, 7)], bb_s.at[0])
    left_here(bb.at[pl.ds(0, 3)], bb_s.at[1])
    for part in range(2):
        for stage in range(4):
            left_here(w_sizes[part][stage], w_s.at[part, stage])
        for stage, ref in rs_sizes[part].items():
            left_here(ref, rs_s.at[part, stage])
    left_here(bgz, bg_s.at[0])
    left_here(bgx, bg_s.at[1])
    left_here(bgf.at[pl.ds(0, 7)], bg_s.at[2])

    @pl.when(ctx == 0)
    def _():
        left_here(kv.at[0, :, pl.ds(0, 3 * SINKS), :], sk.at[0])

    @pl.when(z == 0)
    def _():
        left_here(kv.at[0, :, pl.ds(0, 7 * SINKS), :], sk.at[1])


def write_out(fin_u, fin_d, terms, down_out, up_out, bias_out):
    for b in range(4):
        block = jnp.concatenate([fin_u[p, b // 2, 16 * (b % 2) : 16 * (b % 2) + 16, :] for p in range(N_DP)], axis=0)
        up_out[128 * b : 128 * b + 128, :] = block.astype(F32).T
    for e in range(2):
        block = jnp.concatenate([fin_d[4 * e + n // 2, n % 2] for n in range(8)], axis=0)
        down_out[:, e * HEAD_DIM : (e + 1) * HEAD_DIM] = block.astype(F32)
    bias_out[0] = jnp.sum(terms[0:1, :])
    bias_out[1] = jnp.sum(terms[1:2, :])


def on_device(q, k, v, a, h, bias, windows, counts, down, up):
    hbm, smem, vmem = (pl.BlockSpec(memory_space=s) for s in (pl.ANY, pltpu.SMEM, pltpu.VMEM))
    sem = pltpu.SemaphoreType.DMA
    heads = HEADS * HEAD_DIM

    def pair(*dims):
        return [pltpu.VMEM(dims + (rows, HEAD_DIM), BF16) for rows in (UP_ROWS, DOWN_ROWS)]

    scratch = [
        pltpu.VMEM((BLOCKS, KV_HEADS, TOK, 2 * HEAD_DIM), BF16),
        pltpu.VMEM((KV_HEADS, SINKS, 2 * HEAD_DIM), BF16),
        pltpu.VMEM((NX, NZ, 8, HEAD_DIM), F32),
        *pair(2, 2, NX, NY, NZ),
        pltpu.VMEM((TOK, heads), BF16),
        pltpu.VMEM((TOK, a.shape[2]), BF16),
        pltpu.VMEM((TOK, heads), BF16),
        pltpu.VMEM((TOK, heads), BF16),
        pltpu.VMEM((TOK, heads), F32),
        pltpu.VMEM((HEAD_DIM, COLS), BF16),
        pltpu.VMEM((COLS, 2 * HEAD_DIM), BF16),
        pltpu.VMEM((TOK, BLOCKS * TOK), F32),
        *pair(2, 2, NX, NY, NZ),
        *pair(2, NX, NY, NZ),
        *pair(2, 3, 4, NZ),
        *pair(2, 4, NZ),
        *pair(2, 3, NZ),
        *pair(NZ, 2),
        *pair(NZ - 1, 2),
        *pair(N_DP, 2),
        pltpu.VMEM((NZ, NX, 8, HEAD_DIM), F32),
        pltpu.VMEM((NZ - 1, NX, 8, HEAD_DIM), F32),
        pltpu.VMEM((NX, 8, HEAD_DIM), F32),
        pltpu.VMEM((NX - 1, 8, HEAD_DIM), F32),
        pltpu.VMEM((N_DP, 8, HEAD_DIM), F32),
        sem((6,)),
        sem((1,)),
        sem((BLOCKS, KV_HEADS)),
        sem((3,)),
        sem((2,)),
        sem((2,)),
        sem((2, 4)),
        sem((2, 4)),
        sem((2, 8)),
        sem((2, 8)),
        sem((3,)),
        sem((3,)),
    ]
    reduced = pl.pallas_call(
        kernel,
        out_shape=(
            jax.ShapeDtypeStruct((N_DP, 2, UP_ROWS, HEAD_DIM), BF16),
            jax.ShapeDtypeStruct((N_DP, 2, DOWN_ROWS, HEAD_DIM), BF16),
            jax.ShapeDtypeStruct((8, HEAD_DIM), F32),
        ),
        in_specs=[smem] * 3 + [hbm] * 7,
        out_specs=(vmem, vmem, vmem),
        scratch_shapes=scratch,
        compiler_params=pltpu.CompilerParams(
            collective_id=0, has_side_effects=True, vmem_limit_bytes=60 * 1024 * 1024
        ),
        name="token_parallel",
    )(bias, windows, counts, q, k, v, a, h, down, up)
    return pl.pallas_call(
        write_out,
        out_shape=(
            jax.ShapeDtypeStruct(down.shape, F32),
            jax.ShapeDtypeStruct(up.shape, F32),
            jax.ShapeDtypeStruct(bias.shape, F32),
        ),
        in_specs=[vmem] * 3,
        out_specs=(vmem, vmem, smem),
        name="write_out",
    )(*reduced)


def solution(mesh):
    rows = P("dp", "ctx", None)
    placed = (rows,) * 5 + (P("ctx"), P("dp"), P("dp"), P(None, "ctx"), P("ctx", None))
    return jax.shard_map(
        on_device,
        mesh=mesh,
        in_specs=placed,
        out_specs=(P(None, "ctx"), P("ctx", None), P("ctx")),
        check_vma=False,
    )
```

time: 172 us -> 118 us (0.69)
  Pallas kernels: 165 us -> 116 us
  local copies, waits for them, and re-layouts: 4.35 us -> 0 us
    pallas_call x1 -> x2, Pallas kernels: 165 us -> 116 us  [the longest x1 114 us: on_device(): pl.pallas_call(kernel, out_shape=(jax.ShapeDtypeStruct((N_DP, 2, UP_ROWS,...]
    unnamed x3 -> x0, local copies, waits for them, and re-layouts: 4.35 us -> none
where the time goes in v2:
time: 118 us
  Pallas kernels  116 us (98%)
  between operations  1.93 us (2%)
    pallas_call x1, Pallas kernels, on_device(): pl.pallas_call(kernel, out_shape=(jax.ShapeDtypeStruct((N_DP, 2, UP_ROWS,...  114 us

profile of v2, /device:TPU:1, one launch (start us, length us, event | category | flops | bytes accessed | tf_op | source)
XLA Modules:
  0.0 117.6 jit_solution(10580364936354867937)
XLA Ops:
  1.9 113.9 %token_parallel.1 = (bf16[8,2,32,128]{3,2,1,0:T(8,128)(2,1)}, bf16[8,2,16,128]{3,2,1,0:T(8,128)(2,1)}, f32[8,128]{1,0:T(8,128)}) custom-call(f32[2]{0:T(128)} %bias_ref.1, s32[1]{0:T(128)S(6)} %copy.13.win_ref, s32[1]{0:T(128)S(6)} %copy.14.cnt_ref, bf16[1,128,8192]{2,1,0:T(8,128)(2,1)} %q_hbm.1, bf16[1,128,512]{2,1,0:T(8,128)(2,1)} %k_hbm.1, ...), custom_call_target="tpu_custom_call" | custom-call | tf_op jit(solution)/shard_map/token_parallel/pallas_call | solution.py:600
  115.8 1.8 %write_out.1 = (f32[128,256]{1,0:T(8,128)}, f32[512,128]{1,0:T(8,128)}, f32[2]{0:T(128)}) custom-call(bf16[8,2,32,128]{3,2,1,0:T(8,128)(2,1)} %get-tuple-element.6.fin_u, bf16[8,2,16,128]{3,2,1,0:T(8,128)(2,1)} %get-tuple-element.7.fin_d, f32[8,128]{1,0:T(8,128)} %get-tuple-element.8.terms), custom_call_target="tpu_custom_call" | custom-call | tf_op jit(solution)/shard_map/write_out/pallas_call | solution.py:615

commit v3 on v2

--- a/solution.py
+++ b/solution.py
@@ -24,7 +24,6 @@
 MESH = pl.DeviceIdType.MESH
 
 ORDER = (1, 2, 3, 4, 5, 6, 7, 0, 8)
-MAIN = 7 * TOK
 COLS = 10 * TOK
 
 
@@ -39,7 +38,7 @@
 def kernel(
     bias_ref, win_ref, cnt_ref, q_hbm, k_hbm, v_hbm, a_hbm, h_hbm, dw_hbm, uw_hbm,
     fin_u_out, fin_d_out, bias_out,
-    kv, sink, bb, wu, wd, q_s, a_s, h_s, o_s, t_s, kt, ve, mask,
+    kv, sink, bb, wu, wd, q_s, a_s, h_s, o_s, t_s, kt, ve, mask, score_a, score_b,
     gu, gd, rcu, rcd, rau, rad, s2u, s2d, rbu, rbd, s3u, s3d, r3u, r3d, finu, find,
     bg, bgz, bgs, bgx, bgf,
     ld, kv_s, kv_r, sk, bb_s, bb_r, w_s, w_r, rs_s, rs_r, bg_s, bg_r,
@@ -120,24 +119,19 @@
     def kv_arrived(g, slot):
         arrived(kv.at[slot, g], kv_r.at[slot, g])
 
-    def kv_hop(step):
-        for g in range(KV_HEADS):
-            kv_arrived(g, step)
-            kv_push(g, step, step + 1, right)
-            if step == 1:
-
-                @pl.when(z != 0)
-                def _():
-                    kv_arrived(g, 8)
-                    kv_push(g, 8, 7, left)
-
-            else:
-                kv_arrived(g, 9 - step)
-                kv_push(g, 9 - step, 8 - step, left)
-
-    for g in range(KV_HEADS):
-        kv_push(g, 0, 1, right)
-        kv_push(g, 0, far_slot, far_device)
+    def kv_hop(g, step):
+        kv_arrived(g, step)
+        kv_push(g, step, step + 1, right)
+        if step == 1:
+
+            @pl.when(z != 0)
+            def _():
+                kv_arrived(g, 8)
+                kv_push(g, 8, 7, left)
+
+        else:
+            kv_arrived(g, 9 - step)
+            kv_push(g, 9 - step, 8 - step, left)
 
     def sink_copies(axis):
         if axis == "x":
@@ -150,45 +144,86 @@
             copy.start()
 
     weights = (wd, wu)
+    Z_STAGE, SECOND_STAGE, Y_BELOW, Y_ABOVE, Y_ONWARD, X_BELOW, X_ABOVE, X_ONWARD, SIBLING = range(9)
+    above, below = off(y, 1, NY), off(y, -1, NY)
+    x_above, x_below = off(x, 1, NX), off(x, -1, NX)
+    low, high = pl.ds(0, 2), pl.ds(2, 2)
 
     def w_push(part, stage, src, device):
         push(src, src, w_s.at[part, stage], w_r.at[part, stage], device)
 
-    w_sizes = [
-        (w.at[0, c, 0, pl.ds(0, 2), pl.ds(0, 7)], w.at[0, c, pl.ds(0, 3), pl.ds(0, 2)], w.at[:, c, pl.ds(0, 3)], w.at[:, c])
-        for w in weights
-    ]
+    w_sizes = (
+        {
+            Z_STAGE: wd.at[0, c, 0, low, pl.ds(0, 7)], SECOND_STAGE: wd.at[0, c, pl.ds(0, 3), low],
+            Y_BELOW: wd.at[:, c, 0], Y_ABOVE: wd.at[:, c, 0], Y_ONWARD: wd.at[:, c, 0], SIBLING: wd.at[:, c],
+        },
+        {
+            Z_STAGE: wu.at[0, c, 0, low, pl.ds(0, 7)], SECOND_STAGE: wu.at[0, c, pl.ds(0, 3), low],
+            Y_BELOW: wu.at[0, c, 0], Y_ABOVE: wu.at[0, c, 0], Y_ONWARD: wu.at[0, c, 0],
+            X_BELOW: wu.at[0, c, 0], X_ABOVE: wu.at[0, c, 0], X_ONWARD: wu.at[0, c, 0], SIBLING: wu.at[:, c],
+        },
+    )
 
     def w_arrived(part, stage):
         arrived(w_sizes[part][stage], w_r.at[part, stage])
 
     def along_z(part):
         for i in range(1, NZ):
-            w_push(part, 0, weights[part].at[:, c, x, y, z], dev(z_=off(z, i, NZ)))
+            w_push(part, Z_STAGE, weights[part].at[:, c, x, y, z], dev(z_=off(z, i, NZ)))
 
     def second(part):
         w = weights[part]
+        w_arrived(part, Z_STAGE)
         for i in range(1, NX):
             if part == 0:
-                w_push(part, 1, w.at[:, c, x, y], dev(x_=off(x, i, NX)))
+                w_push(part, SECOND_STAGE, w.at[:, c, x, y], dev(x_=off(x, i, NX)))
             else:
-                w_push(part, 1, w.at[0, c, x, y], dev(x_=off(x, i, NX)))
-                w_push(part, 1, w.at[1, c, x, y], dev(y_=off(y, i, NY)))
-
-    def third(part, half):
+                w_push(part, SECOND_STAGE, w.at[0, c, x, y], dev(x_=off(x, i, NX)))
+                w_push(part, SECOND_STAGE, w.at[1, c, x, y], dev(y_=off(y, i, NY)))
+
+    def rings(part):
         w = weights[part]
-        for i in range(1, NX):
+        w_arrived(part, SECOND_STAGE)
+        for half in range(2):
             if part == 1 and half == 1:
-                w_push(part, 2, w.at[1, c, x], dev(x_=off(x, i, NX)))
+                w_push(part, X_BELOW, w.at[1, c, x], dev(x_=x_above))
+                w_push(part, X_ABOVE, w.at[1, c, x], dev(x_=x_below))
             else:
-                w_push(part, 2, w.at[half, c, :, y], dev(y_=off(y, i, NY)))
-
-    def core(part):
-        w_push(part, 3, weights[part].at[:, c], sibling)
-
+                w_push(part, Y_BELOW, w.at[half, c, :, y], dev(y_=above))
+                w_push(part, Y_ABOVE, w.at[half, c, :, y], dev(y_=below))
+
+    def y_onward(part):
+        w_arrived(part, Y_BELOW)
+        from_below = wd.at[0, c, :, below] if part == 0 else wu.at[0, c, low, below]
+        w_push(part, Y_ONWARD, from_below, dev(y_=above))
+        w_arrived(part, Y_ABOVE)
+        from_above = wd.at[1, c, :, above] if part == 0 else wu.at[0, c, high, above]
+        w_push(part, Y_ONWARD, from_above, dev(y_=below))
+
+    def x_onward(part):
+        w_arrived(part, X_BELOW)
+        w_push(part, X_ONWARD, wu.at[1, c, x_below, low], dev(x_=x_above))
+        w_arrived(part, X_ABOVE)
+        w_push(part, X_ONWARD, wu.at[1, c, x_above, high], dev(x_=x_below))
+
+    def to_sibling(part):
+        w_arrived(part, Y_ONWARD)
+        if part == 1:
+            w_arrived(part, X_ONWARD)
+        w_push(part, SIBLING, weights[part].at[:, c], sibling)
+
+    def spread_jump(g):
+        @pl.when(first_z)
+        def _():
+            kv_push(g, 0, 8, jump)
+
+    along_z(0)
+    for g in range(KV_HEADS):
+        kv_push(g, 0, 1, right)
+        kv_push(g, 0, far_slot, far_device)
+    spread_jump(0)
     for i in range(1, NZ):
         push(bb.at[x, z], bb.at[x, z], bb_s.at[0], bb_r.at[0], dev(z_=off(z, i, NZ)))
-    along_z(0)
     along_z(1)
 
     window, count = win_ref[0], cnt_ref[0]
@@ -202,14 +237,17 @@
     for j in range(7):
         mask[:, j * TOK : (j + 1) * TOK] = jnp.where(seen(ORDER[j]), 0.0, MASKED)
     both = jnp.where(causal, jnp.where(seen(0), 1, 0), jnp.where(seen(8), 1, 0)) == 1
-    mask[:, MAIN : MAIN + TOK] = jnp.where(both, 0.0, MASKED)
+    mask[:, 7 * TOK : 8 * TOK] = jnp.where(both, 0.0, MASKED)
     sink_seen = (col <= ctx * TOK + row) & (col < count)
-    mask[:, MAIN + TOK : MAIN + 2 * TOK] = jnp.where(sink_seen, 0.0, MASKED)
+    mask[:, 8 * TOK :] = jnp.where(sink_seen, 0.0, MASKED)
     ve[:, HEAD_DIM:] = jnp.ones((COLS, HEAD_DIM), BF16)
     ve[BLOCKS * TOK :, 0:HEAD_DIM] = jnp.zeros((TOK, HEAD_DIM), BF16)
     bg[...] = jnp.zeros(bg.shape, F32)
 
-    kv_hop(1)
+    second(0)
+    for g in range(KV_HEADS):
+        kv_hop(g, 1)
+    spread_jump(1)
 
     @pl.when((z == 0) & (x != 0))
     def _():
@@ -223,33 +261,78 @@
     arrived(bb.at[0, pl.ds(0, 7)], bb_r.at[0])
     for i in range(1, NX):
         push(bb.at[x], bb.at[x], bb_s.at[1], bb_r.at[1], dev(x_=off(x, i, NX)))
-    w_arrived(0, 0)
-    second(0)
-
-    kv_hop(2)
-
-    w_arrived(1, 0)
     second(1)
-    w_arrived(0, 1)
-    third(0, 0)
-    third(0, 1)
-
-    kv_hop(3)
-
-    @pl.when(first_z)
-    def _():
-        for g in range(KV_HEADS):
-            kv_push(g, 0, 8, jump)
-
-    w_arrived(1, 1)
-    third(1, 0)
+    rings(0)
+
+    for g in range(KV_HEADS):
+        kv_hop(g, 2)
+    spread_jump(2)
+    rings(1)
+
     arrived(bb.at[pl.ds(0, 3)], bb_r.at[1])
 
     @pl.when(z != 0)
     def _():
         arrived(sink, sk.at[2])
 
+    for g in range(KV_HEADS):
+        kv_hop(g, 3)
+    spread_jump(3)
+    y_onward(0)
     late[0].wait()
+
+    def columns(head):
+        return pl.ds(pl.multiple_of(head * HEAD_DIM, HEAD_DIM), HEAD_DIM)
+
+    rows = HEAD_STEP * TOK
+
+    def score_heads(first, score_s):
+        queries = jnp.concatenate([q_s[:, columns(first + e)] for e in range(HEAD_STEP)], axis=0)
+        score = (dot(queries, kt[...]) * SCORE_SCALE).reshape(HEAD_STEP, TOK, COLS)
+
+        def tile(j):
+            return score[:, :, j * TOK : (j + 1) * TOK]
+
+        biases = []
+        for e in range(HEAD_STEP):
+            shard = (first + e) // 2
+            biases.append(bb[shard // NZ, shard % NZ, e % 2 : e % 2 + 1, :][None])
+        top = None
+        for j in range(BLOCKS):
+            seen_j = mask[:, j * TOK : (j + 1) * TOK][None]
+            if j < 7:
+                part = tile(j) + seen_j
+            elif j == 7:
+                part = jnp.where(causal[None], tile(7), tile(8)) + seen_j
+            else:
+                part = tile(9) + (seen_j + jnp.concatenate(biases, axis=0))
+            score_s[:, :, j * TOK : (j + 1) * TOK] = part
+            top = part if top is None else jnp.maximum(top, part)
+        return jnp.max(top, axis=-1, keepdims=True)
+
+    def finish_heads(first, score_s, top):
+        probs = [jnp.exp2(score_s[:, :, j * TOK : (j + 1) * TOK] - top).astype(BF16) for j in range(BLOCKS)]
+        nothing = jnp.zeros((), BF16)
+        near = jnp.where(causal[None], probs[7], nothing)
+        far = jnp.where(causal[None], nothing, probs[7])
+        local = jnp.concatenate(probs[:7] + [near, far], axis=-1).reshape(rows, BLOCKS * TOK)
+        from_sinks = dot(probs[8].reshape(rows, TOK), ve[BLOCKS * TOK :, :])
+        total = dot(local, ve[0 : BLOCKS * TOK, :]) + from_sinks
+        scale = 1.0 / total[:, HEAD_DIM:]
+        out = (total[:, 0:HEAD_DIM] * scale).astype(BF16)
+        term = (from_sinks[:, 0:HEAD_DIM] - from_sinks[:, HEAD_DIM:] * out.astype(F32)) * scale
+        for e in range(HEAD_STEP):
+            o_s[:, columns(first + e)] = out[e * TOK : (e + 1) * TOK]
+            t_s[:, columns(first + e)] = term[e * TOK : (e + 1) * TOK]
+
+    def attend_heads(first):
+        steps = GROUP // HEAD_STEP
+        held = (score_a, score_b)
+        top = score_heads(first, held[0])
+        for n in range(steps):
+            later = score_heads(first + (n + 1) * HEAD_STEP, held[(n + 1) % 2]) if n + 1 < steps else None
+            finish_heads(first + n * HEAD_STEP, held[n % 2], top)
+            top = later
 
     def attend_group(g, carry):
         kv_arrived(g, 4)
@@ -262,63 +345,23 @@
         for j, block in enumerate(ORDER):
             kt[:, j * TOK : (j + 1) * TOK] = kv[block, g, :, 0:HEAD_DIM].T
             ve[j * TOK : (j + 1) * TOK, 0:HEAD_DIM] = kv[block, g, :, HEAD_DIM:]
-        padded = jnp.concatenate(
-            [sink[g, :, 0:HEAD_DIM], jnp.zeros((TOK - SINKS, HEAD_DIM), BF16)], axis=0
-        )
+        padded = jnp.concatenate([sink[g, :, 0:HEAD_DIM], jnp.zeros((TOK - SINKS, HEAD_DIM), BF16)], axis=0)
         kt[:, BLOCKS * TOK :] = padded.T
         ve[BLOCKS * TOK : BLOCKS * TOK + SINKS, 0:HEAD_DIM] = sink[g, :, HEAD_DIM:]
-
-        def attend_heads(step, carry):
-            first = g * GROUP + step * HEAD_STEP
-            rows = HEAD_STEP * TOK
-
-            def columns(e):
-                return pl.ds(pl.multiple_of((first + e) * HEAD_DIM, HEAD_DIM), HEAD_DIM)
-
-            queries = jnp.concatenate([q_s[:, columns(e)] for e in range(HEAD_STEP)], axis=0)
-            score = dot(queries, kt[...]) * SCORE_SCALE
-            score = score.reshape(HEAD_STEP, TOK, COLS)
-            parts = [
-                score[:, :, j * TOK : (j + 1) * TOK] + mask[:, j * TOK : (j + 1) * TOK][None] for j in range(7)
-            ]
-            edge = jnp.where(causal[None], score[:, :, MAIN : MAIN + TOK], score[:, :, MAIN + TOK : MAIN + 2 * TOK])
-            parts.append(edge + mask[:, MAIN : MAIN + TOK][None])
-            biases = []
-            for e in range(HEAD_STEP):
-                head = first + e
-                shard = head // 2
-                biases.append(bb[shard // NZ, shard % NZ, e % 2 : e % 2 + 1, :])
-            bias = jnp.concatenate([b[None] for b in biases], axis=0)
-            parts.append(score[:, :, BLOCKS * TOK :] + (mask[:, MAIN + TOK : MAIN + 2 * TOK][None] + bias))
-            top = parts[0]
-            for part in parts[1:]:
-                top = jnp.maximum(top, part)
-            top = jnp.max(top, axis=-1, keepdims=True)
-            probs = [jnp.exp2(part - top).astype(BF16) for part in parts]
-            nothing = jnp.zeros((), BF16)
-            near = jnp.where(causal[None], probs[7], nothing)
-            far = jnp.where(causal[None], nothing, probs[7])
-            local = jnp.concatenate(probs[:7] + [near, far], axis=-1).reshape(rows, BLOCKS * TOK)
-            from_sinks = dot(probs[8].reshape(rows, TOK), ve[BLOCKS * TOK :, :])
-            total = dot(local, ve[0 : BLOCKS * TOK, :]) + from_sinks
-            scale = 1.0 / total[:, HEAD_DIM:]
-            out = (total[:, 0:HEAD_DIM] * scale).astype(BF16)
-            term = (from_sinks[:, 0:HEAD_DIM] - from_sinks[:, HEAD_DIM:] * out.astype(F32)) * scale
-            for e in range(HEAD_STEP):
-                o_s[:, columns(e)] = out[e * TOK : (e + 1) * TOK]
-                t_s[:, columns(e)] = term[e * TOK : (e + 1) * TOK]
-            return carry
-
-        lax.fori_loop(0, GROUP // HEAD_STEP, attend_heads, 0)
+        attend_heads(g * GROUP)
 
         @pl.when(g == 0)
         def _():
-            third(1, 1)
+            y_onward(1)
+            x_onward(1)
+
+        @pl.when(g == 1)
+        def _():
+            to_sibling(0)
 
         @pl.when(g == 2)
         def _():
-            w_arrived(0, 2)
-            core(0)
+            to_sibling(1)
 
         return carry
 
@@ -332,7 +375,7 @@
             for e in range(2)
         ]
 
-    w_arrived(0, 3)
+    w_arrived(0, SIBLING)
 
     def low_out_step(xs, total):
         down = jnp.concatenate([w for zs in range(NZ) for w in down_weight(xs, zs)], axis=1)
@@ -440,12 +483,9 @@
         to_core(1, j)
         if j > 0:
             first_stage(1, j - 1)
-        if j == 2:
-            w_arrived(1, 2)
-            core(1)
     first_stage(1, 3)
 
-    w_arrived(1, 3)
+    w_arrived(1, SIBLING)
 
     def low_grad_step(xs, total):
         up = jnp.concatenate(
@@ -522,8 +562,8 @@
     left_here(bb.at[0, pl.ds(0, 7)], bb_s.at[0])
     left_here(bb.at[pl.ds(0, 3)], bb_s.at[1])
     for part in range(2):
-        for stage in range(4):
-            left_here(w_sizes[part][stage], w_s.at[part, stage])
+        for stage, ref in w_sizes[part].items():
+            left_here(ref, w_s.at[part, stage])
         for stage, ref in rs_sizes[part].items():
             left_here(ref, rs_s.at[part, stage])
     left_here(bgz, bg_s.at[0])
@@ -571,6 +611,8 @@
         pltpu.VMEM((HEAD_DIM, COLS), BF16),
         pltpu.VMEM((COLS, 2 * HEAD_DIM), BF16),
         pltpu.VMEM((TOK, BLOCKS * TOK), F32),
+        pltpu.VMEM((HEAD_STEP, TOK, BLOCKS * TOK), F32),
+        pltpu.VMEM((HEAD_STEP, TOK, BLOCKS * TOK), F32),
         *pair(2, 2, NX, NY, NZ),
         *pair(2, NX, NY, NZ),
         *pair(2, 3, 4, NZ),
@@ -590,8 +632,8 @@
         sem((3,)),
         sem((2,)),
         sem((2,)),
-        sem((2, 4)),
-        sem((2, 4)),
+        sem((2, 9)),
+        sem((2, 9)),
         sem((2, 8)),
         sem((2, 8)),
         sem((3,)),

time: 118 us -> 111 us (0.941)
  Pallas kernels: 116 us -> 109 us
    pallas_call x1, Pallas kernels: 114 us -> 107 us  [on_device(): pl.pallas_call(kernel, out_shape=(jax.ShapeDtypeStruct((N_DP, 2, UP_ROWS,...]
where the time goes in v3:
time: 111 us
  Pallas kernels  109 us (98%)
  between operations  1.93 us (2%)
    pallas_call x1, Pallas kernels, on_device(): pl.pallas_call(kernel, out_shape=(jax.ShapeDtypeStruct((N_DP, 2, UP_ROWS,...  107 us

profile of v3, /device:TPU:1, one launch (start us, length us, event | category | flops | bytes accessed | tf_op | source)
XLA Modules:
  0.0 111.1 jit_solution(12367334928998641169)
XLA Ops:
  1.9 107.4 %token_parallel.1 = (bf16[8,2,32,128]{3,2,1,0:T(8,128)(2,1)}, bf16[8,2,16,128]{3,2,1,0:T(8,128)(2,1)}, f32[8,128]{1,0:T(8,128)}) custom-call(f32[2]{0:T(128)} %bias_ref.1, s32[1]{0:T(128)S(6)} %copy.13.win_ref, s32[1]{0:T(128)S(6)} %copy.14.cnt_ref, bf16[1,128,8192]{2,1,0:T(8,128)(2,1)} %q_hbm.1, bf16[1,128,512]{2,1,0:T(8,128)(2,1)} %k_hbm.1, ...), custom_call_target="tpu_custom_call" | custom-call | tf_op jit(solution)/shard_map/token_parallel/pallas_call | solution.py:642
  109.3 1.8 %write_out.1 = (f32[128,256]{1,0:T(8,128)}, f32[512,128]{1,0:T(8,128)}, f32[2]{0:T(128)}) custom-call(bf16[8,2,32,128]{3,2,1,0:T(8,128)(2,1)} %get-tuple-element.6.fin_u, bf16[8,2,16,128]{3,2,1,0:T(8,128)(2,1)} %get-tuple-element.7.fin_d, f32[8,128]{1,0:T(8,128)} %get-tuple-element.8.terms), custom_call_target="tpu_custom_call" | custom-call | tf_op jit(solution)/shard_map/write_out/pallas_call | solution.py:657

commit v4 on v3

--- a/solution.py
+++ b/solution.py
@@ -15,6 +15,7 @@
 RANK = 128
 SINKS = 16
 BLOCKS = 9
+RELAY = 9
 UP_ROWS, DOWN_ROWS = 32, 16
 HEAD_STEP = 4
 MASKED = -1e30
@@ -212,16 +213,10 @@
             w_arrived(part, X_ONWARD)
         w_push(part, SIBLING, weights[part].at[:, c], sibling)
 
-    def spread_jump(g):
-        @pl.when(first_z)
-        def _():
-            kv_push(g, 0, 8, jump)
-
     along_z(0)
     for g in range(KV_HEADS):
         kv_push(g, 0, 1, right)
         kv_push(g, 0, far_slot, far_device)
-    spread_jump(0)
     for i in range(1, NZ):
         push(bb.at[x, z], bb.at[x, z], bb_s.at[0], bb_r.at[0], dev(z_=off(z, i, NZ)))
     along_z(1)
@@ -247,7 +242,12 @@
     second(0)
     for g in range(KV_HEADS):
         kv_hop(g, 1)
-    spread_jump(1)
+
+    @pl.when(z == 1)
+    def _():
+        for g in range(KV_HEADS):
+            kv_push(g, 1, RELAY, jump)
+
 
     @pl.when((z == 0) & (x != 0))
     def _():
@@ -266,8 +266,7 @@
 
     for g in range(KV_HEADS):
         kv_hop(g, 2)
-    spread_jump(2)
-    rings(1)
+
 
     arrived(bb.at[pl.ds(0, 3)], bb_r.at[1])
 
@@ -277,7 +276,14 @@
 
     for g in range(KV_HEADS):
         kv_hop(g, 3)
-    spread_jump(3)
+
+    @pl.when(z == 1)
+    def _():
+        for g in range(KV_HEADS):
+            kv_arrived(g, RELAY)
+            kv_push(g, RELAY, 8, left)
+
+    rings(1)
     y_onward(0)
     late[0].wait()
 
@@ -476,7 +482,7 @@
                         ]
             return carry
 
-        lax.fori_loop(0, NZ, step, 0, unroll=2)
+        lax.fori_loop(0, NZ, step, 0, unroll=4)
 
     for j in range(NX):
         up_row(order[j])
@@ -512,7 +518,7 @@
                 gd[half, cs, xs, ys, zs] = grad[r : r + DOWN_ROWS, e * HEAD_DIM : (e + 1) * HEAD_DIM]
             return carry
 
-        lax.fori_loop(0, NZ, step, 0, unroll=2)
+        lax.fori_loop(0, NZ, step, 0, unroll=4)
 
     for j in range(NX):
         down_row(order[j])
@@ -558,7 +564,16 @@
     last_arrived(0)
     fin_d_out[...] = find[...]
 
-    left_here(kv.at[pl.ds(1, 8)], kv_s.at[0])
+    left_here(kv.at[pl.ds(0, 7)], kv_s.at[0])
+
+    @pl.when(z != 0)
+    def _():
+        left_here(kv.at[7], kv_s.at[0])
+
+    @pl.when(z == 1)
+    def _():
+        left_here(kv.at[pl.ds(0, 2)], kv_s.at[0])
+
     left_here(bb.at[0, pl.ds(0, 7)], bb_s.at[0])
     left_here(bb.at[pl.ds(0, 3)], bb_s.at[1])
     for part in range(2):
@@ -599,7 +614,7 @@
         return [pltpu.VMEM(dims + (rows, HEAD_DIM), BF16) for rows in (UP_ROWS, DOWN_ROWS)]
 
     scratch = [
-        pltpu.VMEM((BLOCKS, KV_HEADS, TOK, 2 * HEAD_DIM), BF16),
+        pltpu.VMEM((BLOCKS + 1, KV_HEADS, TOK, 2 * HEAD_DIM), BF16),
         pltpu.VMEM((KV_HEADS, SINKS, 2 * HEAD_DIM), BF16),
         pltpu.VMEM((NX, NZ, 8, HEAD_DIM), F32),
         *pair(2, 2, NX, NY, NZ),
@@ -628,7 +643,7 @@
         pltpu.VMEM((N_DP, 8, HEAD_DIM), F32),
         sem((6,)),
         sem((1,)),
-        sem((BLOCKS, KV_HEADS)),
+        sem((BLOCKS + 1, KV_HEADS)),
         sem((3,)),
         sem((2,)),
         sem((2,)),

time: 111 us -> 106 us (0.955)
  Pallas kernels: 109 us -> 104 us
    pallas_call x1, Pallas kernels: 107 us -> 102 us  [on_device(): pl.pallas_call(kernel, out_shape=(jax.ShapeDtypeStruct((N_DP, 2, UP_ROWS,...]
where the time goes in v4:
time: 106 us
  Pallas kernels  104 us (98%)
  between operations  1.93 us (2%)
    pallas_call x1, Pallas kernels, on_device(): pl.pallas_call(kernel, out_shape=(jax.ShapeDtypeStruct((N_DP, 2, UP_ROWS,...  102 us

profile of v4, /device:TPU:1, one launch (start us, length us, event | category | flops | bytes accessed | tf_op | source)
XLA Modules:
  0.0 105.8 jit_solution(5210696527666766418)
XLA Ops:
  1.9 102.1 %token_parallel.1 = (bf16[8,2,32,128]{3,2,1,0:T(8,128)(2,1)}, bf16[8,2,16,128]{3,2,1,0:T(8,128)(2,1)}, f32[8,128]{1,0:T(8,128)}) custom-call(f32[2]{0:T(128)} %bias_ref.1, s32[1]{0:T(128)S(6)} %copy.13.win_ref, s32[1]{0:T(128)S(6)} %copy.14.cnt_ref, bf16[1,128,8192]{2,1,0:T(8,128)(2,1)} %q_hbm.1, bf16[1,128,512]{2,1,0:T(8,128)(2,1)} %k_hbm.1, ...), custom_call_target="tpu_custom_call" | custom-call | tf_op jit(solution)/shard_map/token_parallel/pallas_call | solution.py:657
  104.0 1.8 %write_out.1 = (f32[128,256]{1,0:T(8,128)}, f32[512,128]{1,0:T(8,128)}, f32[2]{0:T(128)}) custom-call(bf16[8,2,32,128]{3,2,1,0:T(8,128)(2,1)} %get-tuple-element.6.fin_u, bf16[8,2,16,128]{3,2,1,0:T(8,128)(2,1)} %get-tuple-element.7.fin_d, f32[8,128]{1,0:T(8,128)} %get-tuple-element.8.terms), custom_call_target="tpu_custom_call" | custom-call | tf_op jit(solution)/shard_map/write_out/pallas_call | solution.py:672

commit v5 on v4

--- a/solution.py
+++ b/solution.py
@@ -551,6 +551,33 @@
         push(bgf.at[dp], bgf.at[dp], bg_s.at[2], bg_r.at[2], (off(dp, i, N_DP), ctx))
 
     third_stage(0)
+
+    left_here(kv.at[pl.ds(0, 7)], kv_s.at[0])
+
+    @pl.when(z != 0)
+    def _():
+        left_here(kv.at[7], kv_s.at[0])
+
+    @pl.when(z == 1)
+    def _():
+        left_here(kv.at[pl.ds(0, 2)], kv_s.at[0])
+
+    left_here(bb.at[0, pl.ds(0, 7)], bb_s.at[0])
+    left_here(bb.at[pl.ds(0, 3)], bb_s.at[1])
+    for part in range(2):
+        for stage, ref in w_sizes[part].items():
+            left_here(ref, w_s.at[part, stage])
+        for stage in (CORE, FIRST):
+            left_here(rs_sizes[part][stage], rs_s.at[part, stage])
+
+    @pl.when(ctx == 0)
+    def _():
+        left_here(kv.at[0, :, pl.ds(0, 3 * SINKS), :], sk.at[0])
+
+    @pl.when(z == 0)
+    def _():
+        left_here(kv.at[0, :, pl.ds(0, 7 * SINKS), :], sk.at[1])
+
     last_stage(1)
     last_stage(0)
 
@@ -564,34 +591,12 @@
     last_arrived(0)
     fin_d_out[...] = find[...]
 
-    left_here(kv.at[pl.ds(0, 7)], kv_s.at[0])
-
-    @pl.when(z != 0)
-    def _():
-        left_here(kv.at[7], kv_s.at[0])
-
-    @pl.when(z == 1)
-    def _():
-        left_here(kv.at[pl.ds(0, 2)], kv_s.at[0])
-
-    left_here(bb.at[0, pl.ds(0, 7)], bb_s.at[0])
-    left_here(bb.at[pl.ds(0, 3)], bb_s.at[1])
     for part in range(2):
-        for stage, ref in w_sizes[part].items():
-            left_here(ref, w_s.at[part, stage])
-        for stage, ref in rs_sizes[part].items():
-            left_here(ref, rs_s.at[part, stage])
+        for stage in (SECOND, THIRD, LAST):
+            left_here(rs_sizes[part][stage], rs_s.at[part, stage])
     left_here(bgz, bg_s.at[0])
     left_here(bgx, bg_s.at[1])
     left_here(bgf.at[pl.ds(0, 7)], bg_s.at[2])
-
-    @pl.when(ctx == 0)
-    def _():
-        left_here(kv.at[0, :, pl.ds(0, 3 * SINKS), :], sk.at[0])
-
-    @pl.when(z == 0)
-    def _():
-        left_here(kv.at[0, :, pl.ds(0, 7 * SINKS), :], sk.at[1])
 
 
 def write_out(fin_u, fin_d, terms, down_out, up_out, bias_out):

time: 106 us -> 106 us (level)
  no operation moved by 1% of the time
where the time goes in v5:
time: 106 us
  Pallas kernels  104 us (98%)
  between operations  1.93 us (2%)
    pallas_call x1, Pallas kernels, on_device(): pl.pallas_call(kernel, out_shape=(jax.ShapeDtypeStruct((N_DP, 2, UP_ROWS,...  102 us

profile of v5, /device:TPU:1, one launch (start us, length us, event | category | flops | bytes accessed | tf_op | source)
XLA Modules:
  0.0 105.8 jit_solution(7360954665160927069)
XLA Ops:
  1.9 102.0 %token_parallel.1 = (bf16[8,2,32,128]{3,2,1,0:T(8,128)(2,1)}, bf16[8,2,16,128]{3,2,1,0:T(8,128)(2,1)}, f32[8,128]{1,0:T(8,128)}) custom-call(f32[2]{0:T(128)} %bias_ref.1, s32[1]{0:T(128)S(6)} %copy.13.win_ref, s32[1]{0:T(128)S(6)} %copy.14.cnt_ref, bf16[1,128,8192]{2,1,0:T(8,128)(2,1)} %q_hbm.1, bf16[1,128,512]{2,1,0:T(8,128)(2,1)} %k_hbm.1, ...), custom_call_target="tpu_custom_call" | custom-call | tf_op jit(solution)/shard_map/token_parallel/pallas_call | solution.py:662
  104.0 1.8 %write_out.1 = (f32[128,256]{1,0:T(8,128)}, f32[512,128]{1,0:T(8,128)}, f32[2]{0:T(128)}) custom-call(bf16[8,2,32,128]{3,2,1,0:T(8,128)(2,1)} %get-tuple-element.6.fin_u, bf16[8,2,16,128]{3,2,1,0:T(8,128)(2,1)} %get-tuple-element.7.fin_d, f32[8,128]{1,0:T(8,128)} %get-tuple-element.8.terms), custom_call_target="tpu_custom_call" | custom-call | tf_op jit(solution)/shard_map/write_out/pallas_call | solution.py:677
